TPU v7x, 32 devices: a whole 2x2x4 slice. The times are simulated.
32 devices in a mesh: batch: 16 (over z, x, core), tp: 2 (over y).
Axes of the slice: x: 2, y: 2, z: 4, core: 2. Of those that a mesh axis runs over, the one named last changes fastest.
Arguments:
- inputs: bfloat16 [24576, 768], P(('batch', 'tp')), may hold values from -6 to 6
- cotangent: bfloat16 [24576, 768], P(('batch', 'tp')), may hold values from -6 to 6
- zinc_lengths: int32 [128], P(('batch', 'tp')), may hold values from 8 to 64, as said below
- pubchem_lengths: int32 [64], P(('batch', 'tp')), may hold values from 16 to 256, as said below
- feature_stack: float32 [8, 12, 32, 64], replicated, may hold values from -6 to 6
- train_step: int32 [1], replicated, may hold values from 0 to 999999
- redraw_interval: int32 [1], replicated, may hold values from 1 to 4999
- attn_gain: float32 [768], replicated, may hold values from 0.5 to 1.5
- attn_shift: float32 [768], replicated, may hold values from -1 to 1
- query_weight: bfloat16 [768, 768], replicated, may hold values from -0.21875 to 0.21875
- query_bias: float32 [768], replicated, may hold values from -1 to 1
- key_weight: bfloat16 [768, 768], replicated, may hold values from -0.21875 to 0.21875
- key_bias: float32 [768], replicated, may hold values from -1 to 1
- value_weight: bfloat16 [768, 768], replicated, may hold values from -0.21875 to 0.21875
- value_bias: float32 [768], replicated, may hold values from -1 to 1
- output_weight: bfloat16 [768, 768], replicated, may hold values from -0.625 to 0.625
- output_bias: float32 [768], replicated, may hold values from -1 to 1
- ffn_gain: float32 [768], replicated, may hold values from 0.5 to 1.5
- ffn_shift: float32 [768], replicated, may hold values from -1 to 1
- hidden_weight: bfloat16 [768, 3072], P(None, 'tp'), may hold values from -0.21875 to 0.21875
- hidden_bias: bfloat16 [3072], P('tp'), may hold values from -1 to 1
- return_weight: bfloat16 [3072, 768], P('tp'), may hold values from -0.109375 to 0.109375
- return_bias: float32 [768], replicated, may hold values from -1 to 1
Outputs:
- layer_out: bfloat16 [24576, 768], P(('batch', 'tp'))
- input_grad: bfloat16 [24576, 768], P(('batch', 'tp'))
- grad_attn_gain: float32 [768], replicated
- grad_attn_shift: float32 [768], replicated
- grad_query_weight: float32 [768, 768], replicated
- grad_query_bias: float32 [768], replicated
- grad_key_weight: float32 [768, 768], replicated
- grad_key_bias: float32 [768], replicated
- grad_value_weight: float32 [768, 768], replicated
- grad_value_bias: float32 [768], replicated
- grad_output_weight: float32 [768, 768], replicated
- grad_output_bias: float32 [768], replicated
- grad_ffn_gain: float32 [768], replicated
- grad_ffn_shift: float32 [768], replicated
- grad_hidden_weight: float32 [768, 3072], P(None, 'tp')
- grad_hidden_bias: float32 [3072], P('tp')
- grad_return_weight: float32 [3072, 768], P('tp')
- grad_return_bias: float32 [768], replicated
Inputs may be any that keep to these rules, and one draw needn't show every extreme that they name: `zinc_lengths`: each ZINC molecule has between 8 and 64 live slots. `pubchem_lengths`: each PubChem molecule has between 16 and 256 live slots.
All inputs are finite; a program needn't handle non-finite values.
Results may differ from a plain program's by a relative error of at most 0.018.
Values may be sent and summed in bfloat16 or wider, within the bound.
No kernel may reach another device: no remote copies, remote signals or barrier semaphores. Data moves between devices by JAX's collectives and lax.ppermute only.
A program may use at most 256 MiB of HBM per device.

v0:
```python
import math

import jax
import jax.numpy as jnp
from jax import lax
from jax.sharding import PartitionSpec as P

ZPAD = 64
PPAD = 256


highest_precision = lax.Precision.HIGHEST


def norm_rows(values, gain, shift):
    center = values - jnp.mean(values, axis=-1, keepdims=True)
    spread = jnp.mean(center * center, axis=-1, keepdims=True)
    return center * lax.rsqrt(spread + 1e-05) * gain + shift


def rotary_tables(length, width):
    half = width // 2
    place = jnp.arange(length, dtype=jnp.float32)
    rates = jnp.exp(jnp.arange(half, dtype=jnp.float32) * (-2.0 * math.log(10000.0) / width))
    angles = place[:, None] * rates[None, :]
    return (jnp.cos(angles)[:, None, :], jnp.sin(angles)[:, None, :])


def rotate(values, cosine, sine):
    half = values.shape[-1] // 2
    first = values[..., :half]
    second = values[..., half:]
    return jnp.concatenate(
        [first * cosine - second * sine, second * cosine + first * sine], axis=-1
    )


def positive_features(values, feature_projection):
    scaled_rows = values * values.shape[-1] ** (-0.25)
    inner_product = jnp.einsum(
        "ijrc,rnc->ijrn", scaled_rows, feature_projection, precision=highest_precision
    )
    energy = 0.5 * jnp.sum(scaled_rows * scaled_rows, axis=-1, keepdims=True)
    return jnp.exp(inner_product - energy) * feature_projection.shape[1] ** (-0.5)


def molecule_attention(query, key, value, lengths, feature_projection):
    length = query.shape[1]
    cosine, sine = rotary_tables(length, query.shape[-1])
    query_maps = positive_features(rotate(query, cosine, sine), feature_projection)
    key_maps = positive_features(rotate(key, cosine, sine), feature_projection)
    live = (jnp.arange(length, dtype=jnp.int32)[None, :] < lengths[:, None]).astype(jnp.float32)
    key_maps = key_maps * live[:, :, None, None]
    state = jnp.einsum("gphm,gphd->ghmd", key_maps, value, precision=highest_precision)
    total = jnp.sum(key_maps, axis=1)
    weighted = jnp.einsum("gphm,ghmd->gphd", query_maps, state, precision=highest_precision)
    normaliser = jnp.einsum("gphm,ghm->gph", query_maps, total, precision=highest_precision)
    return weighted / normaliser[..., None]


def attention_core(query, key, value, zinc_lengths, pubchem_lengths, feature_projection):
    heads = feature_projection.shape[0]
    width = query.shape[1] // heads
    zinc_rows = zinc_lengths.shape[0] * ZPAD
    all_rows = query.shape[0]
    zinc_part = molecule_attention(
        query[:zinc_rows].reshape(zinc_lengths.shape[0], ZPAD, heads, width),
        key[:zinc_rows].reshape(zinc_lengths.shape[0], ZPAD, heads, width),
        value[:zinc_rows].reshape(zinc_lengths.shape[0], ZPAD, heads, width),
        zinc_lengths,
        feature_projection,
    )
    pubchem_part = molecule_attention(
        query[zinc_rows:].reshape(pubchem_lengths.shape[0], PPAD, heads, width),
        key[zinc_rows:].reshape(pubchem_lengths.shape[0], PPAD, heads, width),
        value[zinc_rows:].reshape(pubchem_lengths.shape[0], PPAD, heads, width),
        pubchem_lengths,
        feature_projection,
    )
    return jnp.concatenate(
        [
            zinc_part.reshape(zinc_rows, heads * width),
            pubchem_part.reshape(all_rows - zinc_rows, heads * width),
        ],
        axis=0,
    )


def ffn_gelu(values):
    return jax.nn.gelu(values, approximate=False)


def matmul(left, right):
    return jnp.dot(left, right, preferred_element_type=jnp.float32)


def contract_rows(left, right):
    return lax.dot_general(
        left, right, (((0,), (0,)), ((), ())), preferred_element_type=jnp.float32
    )


def contract_cols(left, right):
    return lax.dot_general(
        left, right, (((1,), (1,)), ((), ())), preferred_element_type=jnp.float32
    )


def on_device(
    inputs,
    cotangent,
    zinc_lengths,
    pubchem_lengths,
    feature_stack,
    train_step,
    redraw_interval,
    attn_gain,
    attn_shift,
    query_weight,
    query_bias,
    key_weight,
    key_bias,
    value_weight,
    value_bias,
    output_weight,
    output_bias,
    ffn_gain,
    ffn_shift,
    hidden_weight,
    hidden_bias,
    return_weight,
    return_bias,
):
    pick = train_step[0] // redraw_interval[0] % feature_stack.shape[0]
    feature_projection = lax.dynamic_index_in_dim(feature_stack, pick, 0, keepdims=False)
    rows_in = inputs.astype(jnp.float32)
    normed_one, norm_one_back = jax.vjp(norm_rows, rows_in, attn_gain, attn_shift)
    normed_one_low = normed_one.astype(jnp.bfloat16)
    query = matmul(normed_one_low, query_weight) + query_bias
    key = matmul(normed_one_low, key_weight) + key_bias
    value = matmul(normed_one_low, value_weight) + value_bias

    def attend(query_in, key_in, value_in):
        return attention_core(
            query_in, key_in, value_in, zinc_lengths, pubchem_lengths, feature_projection
        )

    attended, attend_back = jax.vjp(attend, query, key, value)
    attended_low = attended.astype(jnp.bfloat16)
    branch = matmul(attended_low, output_weight) + output_bias
    middle = rows_in + branch
    normed_two, norm_two_back = jax.vjp(norm_rows, middle, ffn_gain, ffn_shift)
    normed_two_low = normed_two.astype(jnp.bfloat16)
    grad_out = cotangent.astype(jnp.float32)
    gathered = lax.all_gather(normed_two_low, "tp", axis=0, tiled=True)
    hidden = matmul(gathered, hidden_weight) + hidden_bias.astype(jnp.float32)
    active, gelu_back = jax.vjp(ffn_gelu, hidden)
    active_low = active.astype(jnp.bfloat16)
    used = active_low
    returned = lax.psum_scatter(
        matmul(used, return_weight).astype(jnp.bfloat16), "tp", scatter_dimension=0, tiled=True
    ).astype(jnp.float32)
    piece = lax.all_gather(cotangent, "tp", axis=0, tiled=True)
    used = active_low
    grad_weight = contract_rows(used, piece)
    grad_rows = contract_cols(piece, return_weight)
    grad_hidden_low = gelu_back(grad_rows)[0].astype(jnp.bfloat16)
    part_hidden_w = contract_rows(gathered, grad_hidden_low)
    part_hidden_b = jnp.sum(grad_hidden_low.astype(jnp.float32), axis=0)
    used = grad_hidden_low
    grad_normed_two = lax.psum_scatter(
        contract_cols(used, hidden_weight).astype(jnp.bfloat16),
        "tp",
        scatter_dimension=0,
        tiled=True,
    ).astype(jnp.float32)
    grad_hidden_weight, grad_hidden_bias, grad_return_weight = (
        lax.psum(part_hidden_w.astype(jnp.bfloat16), "batch").astype(jnp.float32),
        lax.psum(part_hidden_b.astype(jnp.bfloat16), "batch").astype(jnp.float32),
        lax.psum(grad_weight.astype(jnp.bfloat16), "batch").astype(jnp.float32),
    )
    layer_out = (middle + returned + return_bias).astype(jnp.bfloat16)
    grad_return_bias_part = jnp.sum(grad_out, axis=0)
    grad_middle_ffn, grad_ffn_gain_part, grad_ffn_shift_part = norm_two_back(grad_normed_two)
    grad_middle = grad_out + grad_middle_ffn
    grad_branch_low = grad_middle.astype(jnp.bfloat16)
    grad_output_weight_part = contract_rows(attended_low, grad_branch_low)
    grad_output_bias_part = jnp.sum(grad_branch_low.astype(jnp.float32), axis=0)
    grad_attended = contract_cols(grad_branch_low, output_weight)
    grad_query, grad_key, grad_value = attend_back(grad_attended)
    query_gradient_reduced = grad_query.astype(jnp.bfloat16)
    key_grad_low = grad_key.astype(jnp.bfloat16)
    value_gradient_reduced = grad_value.astype(jnp.bfloat16)
    grad_query_weight_part = contract_rows(normed_one_low, query_gradient_reduced)
    grad_key_weight_part = contract_rows(normed_one_low, key_grad_low)
    grad_value_weight_part = contract_rows(normed_one_low, value_gradient_reduced)
    grad_query_bias_part = jnp.sum(query_gradient_reduced.astype(jnp.float32), axis=0)
    grad_key_bias_part = jnp.sum(key_grad_low.astype(jnp.float32), axis=0)
    grad_value_bias_part = jnp.sum(value_gradient_reduced.astype(jnp.float32), axis=0)
    grad_normed_one = (
        contract_cols(query_gradient_reduced, query_weight)
        + contract_cols(key_grad_low, key_weight)
        + contract_cols(value_gradient_reduced, value_weight)
    )
    grad_rows_norm, attention_gain_grad_piece, grad_attn_shift_part = norm_one_back(grad_normed_one)
    input_grad = (grad_middle + grad_rows_norm).astype(jnp.bfloat16)
    shared = lax.psum(
        (
            attention_gain_grad_piece,
            grad_attn_shift_part,
            grad_query_weight_part,
            grad_query_bias_part,
            grad_key_weight_part,
            grad_key_bias_part,
            grad_value_weight_part,
            grad_value_bias_part,
            grad_output_weight_part,
            grad_output_bias_part,
            grad_ffn_gain_part,
            grad_ffn_shift_part,
            grad_return_bias_part,
        ),
        ("batch", "tp"),
    )
    return (
        layer_out,
        input_grad,
        shared[0],
        shared[1],
        shared[2],
        shared[3],
        shared[4],
        shared[5],
        shared[6],
        shared[7],
        shared[8],
        shared[9],
        shared[10],
        shared[11],
        grad_hidden_weight,
        grad_hidden_bias,
        grad_return_weight,
        shared[12],
    )


def solution(mesh):
    return jax.shard_map(
        on_device,
        mesh=mesh,
        in_specs=(
            P(("batch", "tp"), None),
            P(("batch", "tp"), None),
            P(("batch", "tp")),
            P(("batch", "tp")),
            P(),
            P(),
            P(),
            P(),
            P(),
            P(),
            P(),
            P(),
            P(),
            P(),
            P(),
            P(),
            P(),
            P(),
            P(),
            P(None, "tp"),
            P("tp"),
            P("tp", None),
            P(),
        ),
        out_specs=(
            P(("batch", "tp"), None),
            P(("batch", "tp"), None),
            P(),
            P(),
            P(),
            P(),
            P(),
            P(),
            P(),
            P(),
            P(),
            P(),
            P(),
            P(),
            P(None, "tp"),
            P("tp"),
            P("tp", None),
            P(),
        ),
        check_vma=False,
    )
```

profile of v0, /device:TPU:0, one launch (start us, length us, event | category | flops | bytes accessed | tf_op | source)
XLA Modules:
  0.0 642.3 jit_solution(150554430038212135)
XLA Ops:
  24.5 3.0 copy.145
  27.5 3.0 reshape.345
  30.5 3.4 fusion.201
  33.9 3.0 copy.151
  36.9 3.0 reshape.347
  45.3 3.0 copy.148
  48.3 3.3 reshape.346
  53.0 3.5 fusion.99
  56.5 3.2 fusion.194
  66.8 2.7 reshape.366
  69.6 4.9 fusion.199
  74.5 2.7 reshape.367
  77.2 3.1 fusion.198
  88.2 11.1 %reshape.342 = f32[4,64,12,64]{1,0,3,2:T(4,128)} reshape(f32[256,768]{0,1:T(8,128)} %copy.137) | data formatting | bytes 1572864 | tf_op jit(solution)/shard_map/jvp()/reshape | solution.py:69
  100.7 7.4 %fusion.97 = (f32[4,64,12,32]{1,3,0,2:T(8,128)S(1)}, f32[12,32,4,64]{3,1,2,0:T(8,128)}) fusion(f32[4,64,12]{1,0,2:T(4,128)S(1)} %get-tuple-element.155, f32[4,64,12,32]{3,1,0,2:T(8,128)} %copy-done.14, f32[4,64,12,32]{3,1,0,2:T(8,128)} %copy-done.12, f32[8,12,32,64]{3,2,1,0:T(8,128)} %param.27, s32[]{:T(128)S(6)} %select_n.17), kind=kOutput, calls=%fused_computation.180 | convolution fusion | flops 76087296 | bytes 4141060 | tf_op jit(solution)/shard_map/jvp(ijrc,rnc->ijrn)/dot_general | solution.py:40
  108.1 6.5 %fusion.196 = (f32[4,12,32]{2,0,1:T(4,128)S(1)}, f32[4,64,12,32]{1,3,0,2:T(8,128)S(1)}, f32[12,32,4,64]{3,1,2,0:T(8,128)}) fusion(f32[4,64]{1,0:T(4,128)S(1)} %fusion.158, f32[4,64,12]{1,0,2:T(4,128)S(1)} %copy-done.100, f32[4,64,12,32]{3,1,0,2:T(8,128)S(1)} %copy-done.7, f32[4,64,12,32]{3,1,0,2:T(8,128)S(1)} %copy-done.10, f32[8,12,32,64]{3,2,1,0:T(8,128)} %param.27, ...), kind=kOutput, calls=%fused_computation.305 | convolution fusion | flops 76184064 | bytes 1788932 | tf_op jit(solution)/shard_map/jvp(ijrc,rnc->ijrn)/dot_general | solution.py:40
  118.6 4.0 fusion.31
  124.0 2.9 reshape.344
  134.2 38.1 %all-gather.3.cloned.1.call-done = bf16[1536,768]{0,1:T(8,128)(2,1)} async-done(((bf16[768,768]{0,1:T(8,128)(2,1)}), bf16[1536,768]{0,1:T(8,128)(2,1)}) %all-gather.3.cloned.1.call-update) | async-done | bytes 2359312 | tf_op jit(solution)/shard_map/all_gather | solution.py:155
  172.3 26.9 %multiply_convert_fusion = (bf16[1536,1536]{1,0:T(8,128)(2,1)}, f32[1536,1536]{1,0:T(8,128)}, f32[1536,1536]{1,0:T(8,128)}) fusion(f32[1536]{0:T(1024)S(1)} %convert_element_type.98, bf16[1536,768]{0,1:T(8,128)(2,1)} %all-gather.3.cloned.1.call-done, bf16[768,1536]{1,0:T(8,128)(2,1)S(1)} %copy-done), kind=kOutput, calls=%fused_computation.3 | convolution fusion | flops 3779592192 | bytes 28317696 | tf_op jit(solution)/shard_map/dot_general | solution.py:94
  199.3 10.7 %all-gather.5.cloned.1.call-done = bf16[1536,768]{1,0:T(8,128)(2,1)} async-done(((bf16[768,768]{1,0:T(8,128)(2,1)}), bf16[1536,768]{1,0:T(8,128)(2,1)}) %all-gather.5.cloned.1.call-update) | async-done | bytes 2359312 | tf_op jit(solution)/shard_map/all_gather | solution.py:163
  210.0 13.5 %fusion.203 = (bf16[1536]{0:T(1024)(128)(2,1)}, bf16[1536,1536]{1,0:T(8,128)(2,1)S(1)}) fusion(f32[1536,1536]{1,0:T(8,128)} %get-tuple-element.98, f32[1536,1536]{1,0:T(8,128)} %get-tuple-element.174, bf16[1536,768]{1,0:T(8,128)(2,1)} %all-gather.5.cloned.1.call-done, bf16[1536,768]{1,0:T(8,128)(2,1)} %param.44), kind=kOutput, calls=%fused_computation.311 | convolution fusion | flops 3659266560 | bytes 28314624 | tf_op jit(solution)/shard_map/dot_general | solution.py:104
  225.7 5.1 convolution_convert_fusion.2
  232.4 7.7 %convolution_convert_fusion.1 = bf16[768,1536]{1,0:T(8,128)(2,1)} fusion(bf16[1536,768]{0,1:T(8,128)(2,1)S(1)} %copy-done.153, bf16[1536,1536]{1,0:T(8,128)(2,1)} %copy-done.167), kind=kOutput, calls=%fused_computation.31 | convolution fusion | flops 3625058304 | bytes 9437184 | tf_op jit(solution)/shard_map/dot_general | solution.py:98
  240.1 7.5 %convolution_convert_fusion = bf16[1536,768]{1,0:T(8,128)(2,1)} fusion(bf16[1536,1536]{1,0:T(8,128)(2,1)} %get-tuple-element.97, bf16[1536,768]{1,0:T(8,128)(2,1)S(1)} %copy-done.154), kind=kOutput, calls=%fused_computation.30 | convolution fusion | flops 3625058304 | bytes 9437184 | tf_op jit(solution)/shard_map/dot_general | solution.py:98
  252.2 8.5 %convolution_convert_fusion.3 = bf16[1536,768]{0,1:T(8,128)(2,1)} fusion(bf16[1536,1536]{1,0:T(8,128)(2,1)} %get-tuple-element.97, bf16[1536,768]{1,0:T(8,128)(2,1)} %param.44), kind=kOutput, calls=%fused_computation.33 | convolution fusion | flops 3625058304 | bytes 9437184 | tf_op jit(solution)/shard_map/dot_general | solution.py:94
  260.8 4.9 reduce-scatter.5.cloned.1.call-done
  265.6 2.7 convert_reduce_fusion
  275.8 3.1 copy.159
  278.9 3.0 reshape.349
  282.0 3.0 fusion.30
  289.4 3.2 copy.166
  292.6 3.1 fusion.32
  298.4 2.9 convolution_bitcast_fusion
  307.7 3.0 fusion.24
  318.8 3.0 reshape.356
  331.0 4.5 fusion.27
  335.5 4.9 fusion.21
  347.3 3.0 reshape.354
  359.7 3.0 reshape.352
  362.8 4.3 fusion.205
  375.3 34.5 %psum.125 = bf16[1536]{0:T(1024)(128)(2,1)} all-reduce(bf16[1536]{0:T(1024)(128)(2,1)} %get-tuple-element.184), channel_id=1, replica_groups=mesh['batch'=16,'tp'=2] {'batch'}, use_global_device_ids=true, to_apply=%region_44.45 | all-reduce | flops 1536 | bytes 6144 | tf_op jit(solution)/shard_map/psum | solution.py:179
  411.2 4.7 convert_element_type.119
  415.9 2.8 convert_element_type.122
  429.3 5.9 add_convert_fusion.1
  442.4 40.1 %all-reduce.14 = (f32[768]{0:T(1024)}, f32[768]{0:T(1024)}, f32[768]{0:T(1024)}, f32[768]{0:T(1024)}, f32[768]{0:T(1024)}, /*index=5*/f32[768]{0:T(1024)}, f32[768]{0:T(1024)}, f32[768]{0:T(1024)}, f32[768]{0:T(1024)}) all-reduce(f32[768]{0:T(1024)S(1)} %copy-done.144, ...), channel_id=1, replica_groups=mesh['batch'=16,'tp'=2] {'batch','tp'}, use_global_device_ids=true, to_apply=%region_23.24 | all-reduce | flops 6912 | bytes 55296 | tf_op jit(solution)/shard_map/psum | solution.py:207
  482.5 142.7 %all-reduce.20.cloned.1.call-done = (f32[768,768]{1,0:T(8,128)}, f32[768,768]{1,0:T(8,128)}, f32[768,768]{1,0:T(8,128)}, f32[768,768]{1,0:T(8,128)}) async-done(((f32[768,768]{1,0:T(8,128)}, f32[768,768]{1,0:T(8,128)}, f32[768,768]{1,0:T(8,128)}, f32[768,768]{1,0:T(8,128)}), (f32[768,768]{1,0:T(8,128)}, f32[768,768]{1,0:T(8,128)}, f32[768,768]{1,0:T(8,128)}, ...) | async-done | bytes 9437200 | tf_op jit(solution)/shard_map/psum | solution.py:207
  625.2 3.4 copy.361
  (464 shorter events, 146.9 us)
Async XLA Ops:
  7.2 165.2 %copy-start = (bf16[768,1536]{1,0:T(8,128)(2,1)S(1)}, bf16[768,1536]{1,0:T(8,128)(2,1)}, u32[]{:S(2)}) copy-start(bf16[768,1536]{1,0:T(8,128)(2,1)} %param.42) | copy-start | bytes 7077892
  7.2 165.1 %all-gather.3.cloned.1.call-start = ((), (), s32[]{:S(2)}) async-start(), calls=%async_computation.2 | async-start | bytes 3538944 | tf_op jit(solution)/shard_map/all_gather | solution.py:155
  10.4 118.9 %copy-start.4 = (bf16[768,768]{0,1:T(8,128)(2,1)}, bf16[768,768]{0,1:T(8,128)(2,1)S(1)}, u32[]{:S(2)}) copy-start(bf16[768,768]{0,1:T(8,128)(2,1)S(1)} %copy.133) | copy-start | bytes 3538948
  10.6 10.2 %copy-start.120 = (f32[768]{0:T(1024)}, f32[768]{0:T(1024)S(1)}, u32[]{:S(2)}) copy-start(f32[768]{0:T(1024)S(1)} %broadcast_multiply_fusion.5) | copy-start | bytes 9220
  12.1 8.8 %copy-start.132 = (f32[768]{0:T(1024)}, f32[768]{0:T(1024)S(1)}, u32[]{:S(2)}) copy-start(f32[768]{0:T(1024)S(1)} %fusion.153) | copy-start | bytes 9220
  56.5 5.8 copy-start.35
  56.5 4.3 copy-start.20
  59.7 5.2 copy-start.56
  59.7 5.2 copy-start.118
  60.8 4.1 copy-start.113
  100.7 7.4 %copy-start.104 = (f32[4,64,12]{1,0,2:T(4,128)}, f32[4,64,12]{1,0,2:T(4,128)S(1)}, u32[]{:S(2)}) copy-start(f32[4,64,12]{1,0,2:T(4,128)S(1)} %get-tuple-element.155) | copy-start | bytes 36868
  100.7 7.4 %copy-start.7 = (f32[4,64,12,32]{3,1,0,2:T(8,128)S(1)}, f32[4,64,12,32]{3,1,0,2:T(8,128)}, u32[]{:S(2)}) copy-start(f32[4,64,12,32]{3,1,0,2:T(8,128)} %copy-done.6) | copy-start | bytes 1179652
  100.7 7.4 %copy-start.10 = (f32[4,64,12,32]{3,1,0,2:T(8,128)S(1)}, f32[4,64,12,32]{3,1,0,2:T(8,128)}, u32[]{:S(2)}) copy-start(f32[4,64,12,32]{3,1,0,2:T(8,128)} %copy-done.9) | copy-start | bytes 1179652
  100.7 7.4 %copy-start.100 = (f32[4,64,12]{1,0,2:T(4,128)S(1)}, f32[4,64,12]{1,0,2:T(4,128)}, u32[]{:S(2)}) copy-start(f32[4,64,12]{1,0,2:T(4,128)} %get-tuple-element.151) | copy-start | bytes 36868
  108.1 10.5 %copy-start.33 = (f32[4,64,12,32]{1,3,0,2:T(8,128)}, f32[4,64,12,32]{1,3,0,2:T(8,128)S(1)}, u32[]{:S(2)}) copy-start(f32[4,64,12,32]{1,3,0,2:T(8,128)S(1)} %get-tuple-element.163) | copy-start | bytes 1179652
  108.1 7.9 %copy-start.18 = (f32[4,64,12,64]{1,0,3,2:T(4,128)S(1)}, f32[4,64,12,64]{1,0,3,2:T(4,128)}, u32[]{:S(2)}) copy-start(f32[4,64,12,64]{1,0,3,2:T(4,128)} %reshape.342) | copy-start | bytes 2359300
  114.6 7.9 %copy-start.52 = (f32[4,64,12,32]{1,3,0,2:T(8,128)}, f32[4,64,12,32]{1,3,0,2:T(8,128)S(1)}, u32[]{:S(2)}) copy-start(f32[4,64,12,32]{1,3,0,2:T(8,128)S(1)} %get-tuple-element.102) | copy-start | bytes 1179652
  114.6 7.9 %copy-start.98 = (f32[4,12,32]{2,0,1:T(4,128)}, f32[4,12,32]{2,0,1:T(4,128)S(1)}, u32[]{:S(2)}) copy-start(f32[4,12,32]{2,0,1:T(4,128)S(1)} %get-tuple-element.101) | copy-start | bytes 18436
  116.0 6.5 %copy-start.115 = (f32[4,12,1,64]{3,1,0,2:T(8,128)}, f32[4,12,1,64]{3,1,0,2:T(8,128)S(1)}, u32[]{:S(2)}) copy-start(f32[4,12,1,64]{3,1,0,2:T(8,128)S(1)} %copy.349) | copy-start | bytes 36868
  118.5 4.0 copy-start.79
  124.0 5.2 copy-start.164
  133.4 76.6 %all-gather.5.cloned.1.call-start = ((), (), s32[]{:S(2)}) async-start(), calls=%async_computation.4 | async-start | bytes 3538944 | tf_op jit(solution)/shard_map/all_gather | solution.py:163
  134.2 131.5 %reduce-scatter.5.cloned.1.call-start = ((), (), s32[]{:S(2)}) async-start(), calls=%async_computation.5 | async-start | bytes 3538944 | tf_op jit(solution)/shard_map/reduce_scatter | solution.py:171
  230.8 180.4 %all-reduce.22.cloned.1.call-start = ((), (), s32[]{:S(2)}) async-start(), calls=%async_computation.7 | async-start | bytes 9437184 | tf_op jit(solution)/shard_map/psum | solution.py:178
  232.4 7.7 %copy-start.154 = (bf16[1536,768]{1,0:T(8,128)(2,1)S(1)}, bf16[1536,768]{1,0:T(8,128)(2,1)}, u32[]{:S(2)}) copy-start(bf16[1536,768]{1,0:T(8,128)(2,1)} %all-gather.5.cloned.1.call-done) | copy-start | bytes 7077892
  247.7 181.6 %reduce-scatter.3.cloned.1.call-start = ((), (), s32[]{:S(2)}) async-start(), calls=%async_computation.3 | async-start | bytes 3538944 | tf_op jit(solution)/shard_map/reduce_scatter | solution.py:160
  249.5 21.4 %copy-start.44 = (bf16[768,768]{0,1:T(8,128)(2,1)}, bf16[768,768]{0,1:T(8,128)(2,1)S(1)}, u32[]{:S(2)}) copy-start(bf16[768,768]{0,1:T(8,128)(2,1)S(1)} %copy.157) | copy-start | bytes 3538948
  260.7 5.0 copy-start.3
  260.7 364.5 %all-reduce.20.cloned.1.call-start = ((), (), s32[]{:S(2)}) async-start(), calls=%async_computation.6 | async-start | bytes 18874368 | tf_op jit(solution)/shard_map/psum | solution.py:207
  281.9 4.2 copy-start.36
  295.7 5.5 copy-start.22
  331.0 4.5 copy-start.8
  331.0 4.5 copy-start.11
  331.0 4.5 copy-start.123
  335.5 4.9 copy-start.91
  335.5 4.9 copy-start.93
  344.7 5.6 copy-start.70
  362.8 4.4 copy-start.5
  362.8 4.4 copy-start.26
  362.8 4.4 copy-start.49
  362.8 4.4 copy-start.121
  362.8 4.4 copy-start.129
  362.8 4.4 copy-start.133
  362.8 4.4 copy-start.166
  411.2 4.7 copy-start.81
  435.3 4.0 copy-start.28
  435.3 4.0 copy-start.51
  631.1 3.9 copy-start.1
  (127 other events, 300.0 us)
Sparse Core Ops, SparseCore 0:
  133.5 38.7 all-gather.2
  173.9 36.0 all-gather.4
  230.9 34.7 reduce-scatter.4
  270.2 117.3 all-reduce.21
  390.3 34.5 reduce-scatter.2
  432.2 192.9 all-reduce.19
where the time goes:
time: 652 us; the launch traced here: 642 us
  waiting for transfers between devices  197 us (30%)
  matrix products  156 us (24%)
  local copies, waits for them, and re-layouts  137 us (21%)
  blocking collectives  74.6 us (11%)
  other arithmetic  59.2 us (9%)
  between operations  17.8 us (3%)
    psum x1, waiting for transfers between devices, on_device(): lax.psum((attention_gain_grad_piece, grad_attn_shift_part, grad_query_wei...  143 us
    dot_general x6, matrix products, matmul(): return jnp.dot(left, right, preferred_element_type=jnp.float32)  40.8 us
    unnamed x349, local copies, waits for them, and re-layouts  40.7 us
    psum x1, blocking collectives, on_device(): lax.psum((attention_gain_grad_piece, grad_attn_shift_part, grad_query_wei...  40.1 us
    all_gather x1, waiting for transfers between devices, on_device(): gathered = lax.all_gather(normed_two_low, 'tp', axis=0, tiled=True)  38.1 us
    dot_general x8, matrix products, positive_features(): jnp.einsum('ijrc,rnc->ijrn', scaled_rows, feature_projection, precision=h...  35.6 us
    psum x1, blocking collectives, on_device(): lax.psum(part_hidden_b.astype(jnp.bfloat16), 'batch').astype(jnp.float32)  34.5 us
    dot_general x6, matrix products, contract_rows(): lax.dot_general(left, right, (((0,), (0,)), ((), ())), preferred_element_...  27.6 us
  transfers between devices with their start and end apart: 6, of which 4 were waited for; matrix products, arithmetic and copies ran while one was open for 29% of the time, Pallas kernels for 0%

commit v1 on v0

v1 whole, which is shorter than its diff:
```python
import math
import functools
import jax, jax.numpy as jnp, numpy as np
from jax import lax
from jax.experimental import pallas as pl
from jax.experimental.pallas import tpu as pltpu
from jax.sharding import PartitionSpec as P

ZPAD = 64
PPAD = 256
F32 = jnp.float32
BF = jnp.bfloat16
VM = pltpu.VMEM
GROUP = 4

def dot(a, b):
    return jnp.dot(a, b, preferred_element_type=F32)

def dot_t(a, b):
    return lax.dot_general(a, b, (((1,), (1,)), ((), ())), preferred_element_type=F32)

def dot_c(a, b):
    return lax.dot_general(a, b, (((0,), (0,)), ((), ())), preferred_element_type=F32)

def split(v):
    hi = v.astype(BF)
    return hi, (v - hi.astype(F32)).astype(BF)

def norm_parts(values):
    center = values - jnp.mean(values, axis=-1, keepdims=True)
    rate = lax.rsqrt(jnp.mean(center * center, axis=-1, keepdims=True) + 1e-05)
    return center * rate, rate

def row(ref):
    return ref[...].reshape(1, -1)

def block_mask(width):
    f = lax.broadcasted_iota(jnp.int32, (128, width), 0) // 32
    c = lax.broadcasted_iota(jnp.int32, (128, width), 1) % 256 // 64
    return f == c

def molecules(zm, pm):
    return [(i * ZPAD, ZPAD) for i in range(zm)] + [(zm * ZPAD + i * PPAD, PPAD) for i in range(pm)]

def attend_fwd_kernel(zm, pm, zlen, plen, x, gain, shift, wq, wk, wv, bq, bk, bv, wo, bo, gain2, shift2,
                      proj_hi, proj_lo, energy, cos, sin,
                      n1_o, n1t_o, xq_o, xk_o, v_o, fq_o, fk_o, state_o, att_o, attt_o, middle_o, n2_o, n2t_o):
    mols = molecules(zm, pm)
    rows = x.shape[0]
    blocks = []
    start = 0
    while start < rows:
        blocks.append([(i, r, n) for i, (r, n) in enumerate(mols) if start <= r < start + PPAD])
        start += PPAD
    normed, _ = norm_parts(x[...].astype(F32))
    n1_all = (normed * row(gain) + row(shift)).astype(BF)
    n1_o[...] = n1_all
    n1t_o[...] = n1_all.T
    groups = wq.shape[1] // 256
    keep = block_mask(512)
    ones = jnp.ones((PPAD, 256), BF)
    for b, mem in enumerate(blocks):
        rs = slice(b * PPAD, (b + 1) * PPAD)
        n1 = n1_o[rs, :]
        cosb = jnp.concatenate([cos[:n, :] for _, _, n in mem], axis=0)
        sinb = jnp.concatenate([sin[:n, :] for _, _, n in mem], axis=0)
        cosb = jnp.concatenate([cosb, cosb], axis=1)
        sinb = jnp.concatenate([sinb, sinb], axis=1)
        live = []
        for i, r, n in mem:
            limit = zlen[i] if i < zm else plen[i - zm]
            live.append((lax.broadcasted_iota(jnp.int32, (n, 128), 0) < limit).astype(F32))
        live = jnp.concatenate(live, axis=0)
        for g in range(groups):
            cs = slice(g * 256, (g + 1) * 256)
            fs = slice(g * 128, (g + 1) * 128)

            def features(w, bias, x_o):
                v = dot(n1, w[:, cs]) + row(bias)[:, cs]
                x_o[rs, cs] = v.astype(BF)
                ch, cl = split(v * cosb)
                sh, sl = split(v * sinb)
                eh, el = split(v * v)
                ph, plo = proj_hi[g], proj_lo[g]
                e = energy[...]
                inner = (dot_t(ch, ph[:, :256]) + dot_t(sh, ph[:, 256:]) + dot_t(cl, ph[:, :256]) + dot_t(sl, ph[:, 256:])
                         + dot_t(ch, plo[:, :256]) + dot_t(sh, plo[:, 256:]) - dot_t(eh, e) - dot_t(el, e))
                return jnp.exp(inner) * (32 ** -0.5)

            fq = features(wq, bq, xq_o).astype(BF)
            fk = (features(wk, bk, xk_o) * live).astype(BF)
            fq_o[rs, fs] = fq
            fk_o[rs, fs] = fk
            v = (dot(n1, wv[:, cs]) + row(bv)[:, cs]).astype(BF)
            v_o[rs, cs] = v
            for i, r, n in mem:
                off = r - b * PPAD
                ms = slice(off, off + n)
                vo = jnp.concatenate([v[ms], ones[:n]], axis=1)
                state = jnp.where(keep, dot_c(fk[ms], vo), 0.0).astype(BF)
                state_o[i, g] = state
                nd = dot(fq[ms], state)
                att = (nd[:, :256] / nd[:, 256:]).astype(BF)
                att_o[slice(r, r + n), cs] = att
        middle = x[rs, :].astype(F32) + (dot(att_o[rs, :], wo[...]) + row(bo))
        middle_o[rs, :] = middle
        normed, _ = norm_parts(middle)
        n2_o[rs, :] = (normed * row(gain2) + row(shift2)).astype(BF)
    attt_o[...] = att_o[...].T
    n2t_o[...] = n2_o[...].T

def rotary_const():
    place = np.arange(PPAD, dtype=np.float64)
    rates = np.exp(np.arange(32, dtype=np.float64) * (-2.0 * math.log(10000.0) / 64))
    ang = place[:, None] * rates[None, :]
    return (np.tile(np.cos(ang), (1, 4)).astype(np.float32), np.tile(np.sin(ang), (1, 4)).astype(np.float32))

def projection_blocks(fp):
    heads, m, hd = fp.shape
    s = hd ** -0.25
    turned = jnp.concatenate([fp[..., hd // 2:], -fp[..., :hd // 2]], axis=-1)
    eye = jnp.eye(GROUP, dtype=F32)
    def blocks(p):
        p = (p * s).reshape(heads // GROUP, GROUP, m, 1, hd) * eye[None, :, None, :, None]
        return p.reshape(heads // GROUP, GROUP * m, GROUP * hd)
    both = jnp.concatenate([blocks(fp), blocks(turned)], axis=-1)
    return split(both)

def energy_const():
    f = np.arange(128)[:, None] // 32
    c = np.arange(256)[None, :] // 64
    return ((f == c) / 16.0).astype(jnp.bfloat16)

def attend_fwd(x, zlen, plen, gain, shift, wq, bq, wk, bk, wv, bv, wo, bo, gain2, shift2, proj_hi, proj_lo, cos, sin):
    rows, d = x.shape
    zm, pm = zlen.shape[0], plen.shape[0]
    groups = d // 256
    S = jax.ShapeDtypeStruct
    vm = pl.BlockSpec(memory_space=VM)
    sm = pl.BlockSpec(memory_space=pltpu.SMEM)
    outs = (S((rows, d), BF), S((d, rows), BF), S((rows, d), BF), S((rows, d), BF), S((rows, d), BF),
            S((rows, d // 2), BF), S((rows, d // 2), BF), S((zm + pm, groups, 128, 512), BF),
            S((rows, d), BF), S((d, rows), BF), S((rows, d), F32), S((rows, d), BF), S((d, rows), BF))
    return pl.pallas_call(
        functools.partial(attend_fwd_kernel, zm, pm),
        out_shape=outs,
        in_specs=[sm, sm] + [vm] * 18,
        out_specs=(vm,) * len(outs),
        compiler_params=pltpu.CompilerParams(vmem_limit_bytes=40 * 2**20),
        cost_estimate=pl.CostEstimate(flops=2 * 768**3 * 5, bytes_accessed=12 * 2**20, transcendentals=10**6),
        name="attend_fwd",
    )(zlen, plen, x, gain, shift, wq, wk, wv, bq, bk, bv, wo, bo, gain2, shift2, proj_hi, proj_lo, energy_const(), cos, sin)

SQRT_HALF = math.sqrt(0.5)

def gelu_parts(h):
    bell = jnp.exp(h * h * -0.5)
    t = 1.0 / (1.0 + (0.3275911 * SQRT_HALF) * jnp.abs(h))
    poly = t * (0.127414796 + t * (-0.142248368 + t * (0.7107068705 + t * (-0.7265760135 + t * 0.5307027145))))
    tail = poly * bell
    phi = jnp.where(h >= 0, 1.0 - tail, tail)
    return h * phi, phi + h * bell * (1.0 / math.sqrt(2 * math.pi))

def store_relative(out, value, cs, code, pieces):
    step = value.shape[0] // pieces
    for p in range(pieces):
        off = pl.multiple_of(jnp.bitwise_xor(p, code) * step, 16)
        out[pl.ds(off, step), cs] = value[p * step:(p + 1) * step]

def ffn_kernel(pieces, count, at, meta, n2, n2t, cot, cott, hb, *refs):
    hws, rws, refs = refs[:count], refs[count:2 * count], refs[2 * count:]
    send_o, keep_o, act_o, gh_o, bias_o = refs[:5]
    left, right = refs[-2:]
    width = act_o.shape[1]
    tile = 256 if width % 256 == 0 else 128
    if count > 1:
        hw, rw = refs[5:7]
        quarter = meta[4]
        for src, dst in ((hws, hw), (rws, rw)):
            step = src[0].shape[0]
            for p in range(count):
                off = pl.multiple_of(jnp.bitwise_xor(p, quarter) * step, 16)
                dst[pl.ds(off, step), :] = src[p][...]
    else:
        hw, rw = hws[0], rws[0]
    left[0] = n2t[...]
    left[1] = cott[...]
    for c in range(0, width, tile):
        cs = slice(c, c + tile)
        ws = slice(at * width + c, at * width + c + tile)
        h = dot(n2[...], hw[:, ws]) + hb[...].reshape(1, -1)[:, cs].astype(F32)
        act, slope = gelu_parts(h)
        ga = dot_t(cot[...], rw[ws, :])
        gh = (ga * slope).astype(BF)
        act = act.astype(BF)
        act_o[:, cs] = act
        gh_o[:, cs] = gh
        right[0, :, cs] = gh
        right[1, :, cs] = act
        bias_o[:, cs] = jnp.sum(gh.astype(F32), axis=0, keepdims=True)
    me, code = meta[0], meta[1]
    for c in range(0, width, tile):
        cs = slice(c, c + tile)
        store_relative(send_o, dot(left[1 - me], right[1 - me, :, cs]).astype(BF), cs, code, pieces)
        store_relative(keep_o, dot(left[me], right[me, :, cs]).astype(BF), cs, code, pieces)

def ffn_chunk(meta, pieces, n2, n2t, cot, cott, hws, rws, hb, at):
    rows, d = n2.shape
    count = len(hws)
    width = hb.shape[0]
    S = jax.ShapeDtypeStruct
    vm = pl.BlockSpec(memory_space=VM)
    outs = (S((d, width), BF), S((d, width), BF), S((rows, width), BF), S((rows, width), BF), S((1, width), F32))
    if count > 1:
        outs += (S((d, width), BF), S((width, d), BF))
    return pl.pallas_call(
        functools.partial(ffn_kernel, pieces, count, at), out_shape=outs,
        in_specs=[pl.BlockSpec(memory_space=pltpu.SMEM)] + [vm] * (5 + 2 * count), out_specs=(vm,) * len(outs),
        scratch_shapes=[VM((2, d, rows), BF), VM((2, rows, width), BF)],
        compiler_params=pltpu.CompilerParams(vmem_limit_bytes=32 * 2**20),
        cost_estimate=pl.CostEstimate(flops=2 * rows * d * width * 4, bytes_accessed=6 * 2**20, transcendentals=10**6),
        name="ffn_chunk",
    )(meta, n2, n2t, cot, cott, hb, *hws, *rws)

def mid_kernel(k, *refs):
    ghs, hws = refs[:k], refs[k:2 * k]
    middle, cot, wo, gain2, gm_o, gb_o, gatt_o, vec_o = refs[2 * k:]
    rows = middle.shape[0]
    acc_g = acc_s = acc_b = acc_c = 0.0
    for r in range(0, rows, 256):
        rs = slice(r, r + 256)
        e = sum(dot_t(gh[rs, :], hw[...]) for gh, hw in zip(ghs, hws))
        n, rate = norm_parts(middle[rs, :])
        c = cot[rs, :].astype(F32)
        acc_g += jnp.sum(e * n, axis=0, keepdims=True)
        acc_s += jnp.sum(e, axis=0, keepdims=True)
        acc_c += jnp.sum(c, axis=0, keepdims=True)
        eg = e * row(gain2)
        gm = c + rate * (eg - jnp.mean(eg, axis=-1, keepdims=True) - n * jnp.mean(eg * n, axis=-1, keepdims=True))
        gm_o[rs, :] = gm
        gb = gm.astype(BF)
        gb_o[rs, :] = gb
        acc_b += jnp.sum(gb.astype(F32), axis=0, keepdims=True)
        gatt_o[rs, :] = dot_t(gb, wo[...])
    vec_o[...] = jnp.concatenate([acc_g, acc_s, acc_b, acc_c] + [jnp.zeros_like(acc_g)] * 4, axis=0)

def mid(ghs, hws, middle, cot, wo, gain2):
    rows, d = middle.shape
    k = len(ghs)
    S = jax.ShapeDtypeStruct
    vm = pl.BlockSpec(memory_space=VM)
    outs = (S((rows, d), F32), S((rows, d), BF), S((rows, d), F32), S((8, d), F32))
    return pl.pallas_call(
        functools.partial(mid_kernel, k), out_shape=outs,
        in_specs=[vm] * (2 * k + 4), out_specs=(vm,) * 4,
        compiler_params=pltpu.CompilerParams(vmem_limit_bytes=40 * 2**20),
        cost_estimate=pl.CostEstimate(flops=2 * rows * d * (sum(h.shape[1] for h in hws) + 2 * d), bytes_accessed=20 * 2**20, transcendentals=10**4),
        name="mid",
    )(*ghs, *hws, middle, cot, wo, gain2)

def attend_bwd_kernel(zm, pm, pieces, meta, zlen, plen, gatt, gb, xq, xk, v, fq, fk, state, n1t, attt, proj, energy, cos, sin,
                      gq_o, gk_o, gv_o, send_a, keep_a, send_b, keep_b, vec_o, left, right):
    mols = molecules(zm, pm)
    rows, d = gatt.shape
    s2 = 64 ** -0.5
    groups = d // 256
    keep = block_mask(512)
    zero = jnp.zeros((1, 256), F32)
    for g in range(groups):
        cs = slice(g * 256, (g + 1) * 256)
        fs = slice(g * 128, (g + 1) * 128)
        sums = [0.0, 0.0, 0.0]
        for b in range(0, rows, PPAD):
            mem = [(i, r, n) for i, (r, n) in enumerate(mols) if b <= r < b + PPAD]
            gfq, gfk = [], []
            for i, r, n in mem:
                ms = slice(r, r + n)
                st = state[i, g]
                q, k, val = fq[ms, fs], fk[ms, fs], v[ms, cs]
                nd = dot(q, st)
                rden = 1.0 / nd[:, 256:]
                u = gatt[ms, cs] * rden
                w = u * (nd[:, :256] * rden)
                uw = jnp.concatenate([u, -w], axis=1).astype(BF)
                gfq.append(dot_t(uw, st))
                gst = jnp.where(keep, dot_c(q, uw), 0.0).astype(BF)
                val1 = jnp.concatenate([val, jnp.ones((n, 256), BF)], axis=1)
                gv = dot(k, gst[:, :256]).astype(BF)
                gv_o[ms, cs] = gv
                gfk.append(dot_t(val1, gst))
            rs = slice(b, b + PPAD)
            cosb = jnp.concatenate([cos[:n, :] for _, _, n in mem], axis=0)
            sinb = jnp.concatenate([sin[:n, :] for _, _, n in mem], axis=0)
            cosb = jnp.concatenate([cosb, cosb], axis=1)
            sinb = jnp.concatenate([sinb, sinb], axis=1)
            for t, (gf, f, x, o) in enumerate(((gfq, fq, xq, gq_o), (gfk, fk, xk, gk_o))):
                gp = (jnp.concatenate(gf, axis=0) * f[rs, fs].astype(F32)).astype(BF)
                back = dot(gp, proj[g])
                tot = dot(gp, energy[...])
                grad = (cosb * back[:, :256] + sinb * back[:, 256:] - tot * x[rs, cs].astype(F32)).astype(BF)
                o[rs, cs] = grad
                sums[t] += jnp.sum(grad.astype(F32), axis=0, keepdims=True)
            sums[2] += jnp.sum(gv_o[rs, cs].astype(F32), axis=0, keepdims=True)
        vec_o[:, cs] = jnp.concatenate(sums + [zero] * 5, axis=0)
    left[0] = attt[...]
    left[1] = n1t[...]
    right[0] = gb[...]
    right[1] = gv_o[...]
    right[2] = gq_o[...]
    right[3] = gk_o[...]
    me = meta[0]
    half = d // 2
    for lane in range(2):
        code = meta[2 + lane]
        for c in range(0, half, 128):
            cs, to = slice(lane * half + c, lane * half + c + 128), slice(lane * half + c, lane * half + c + 128)
            store_relative(send_a, dot(left[1 - me], right[1 - me, :, cs]).astype(BF), to, code, pieces)
            store_relative(keep_a, dot(left[me], right[me, :, cs]).astype(BF), to, code, pieces)
            store_relative(send_b, dot(left[1], right[3 - me, :, cs]).astype(BF), to, code, pieces)
            store_relative(keep_b, dot(left[1], right[2 + me, :, cs]).astype(BF), to, code, pieces)

def attend_bwd(meta, n_pair, zlen, plen, gatt, gb, xq, xk, v, fq, fk, state, n1t, attt, proj, cos, sin):
    rows, d = gatt.shape
    zm, pm = zlen.shape[0], plen.shape[0]
    S = jax.ShapeDtypeStruct
    vm = pl.BlockSpec(memory_space=VM)
    sm = pl.BlockSpec(memory_space=pltpu.SMEM)
    outs = (S((rows, d), BF),) * 3 + (S((d, d), BF),) * 4 + (S((8, d), F32),)
    return pl.pallas_call(
        functools.partial(attend_bwd_kernel, zm, pm, 2 ** n_pair), out_shape=outs,
        in_specs=[sm] * 3 + [vm] * 14, out_specs=(vm,) * 8,
        scratch_shapes=[VM((2, d, rows), BF), VM((4, rows, d), BF)],
        compiler_params=pltpu.CompilerParams(vmem_limit_bytes=40 * 2**20),
        cost_estimate=pl.CostEstimate(flops=2 * d**3 * 6, bytes_accessed=12 * 2**20, transcendentals=10**6),
        name="attend_bwd",
    )(meta, zlen, plen, gatt, gb, xq, xk, v, fq, fk, state, n1t, attt, proj, back_energy_const(), cos, sin)

def back_energy_const():
    f = np.arange(128)[:, None] // 32
    c = np.arange(256)[None, :] // 64
    return ((f == c) * 64 ** -0.5).astype(jnp.bfloat16)

def input_kernel(gq, gk, gv, wq, wk, wv, x, gm, gain, out_o, vec_o):
    rows = x.shape[0]
    acc_g = acc_s = 0.0
    for r in range(0, rows, 256):
        rs = slice(r, r + 256)
        e = dot_t(gq[rs, :], wq[...]) + dot_t(gk[rs, :], wk[...]) + dot_t(gv[rs, :], wv[...])
        n, rate = norm_parts(x[rs, :].astype(F32))
        acc_g += jnp.sum(e * n, axis=0, keepdims=True)
        acc_s += jnp.sum(e, axis=0, keepdims=True)
        eg = e * row(gain)
        gx = rate * (eg - jnp.mean(eg, axis=-1, keepdims=True) - n * jnp.mean(eg * n, axis=-1, keepdims=True))
        out_o[rs, :] = (gm[rs, :] + gx).astype(BF)
    vec_o[...] = jnp.concatenate([acc_g, acc_s] + [jnp.zeros_like(acc_g)] * 6, axis=0)

def input_back(gq, gk, gv, wq, wk, wv, x, gm, gain):
    rows, d = x.shape
    S = jax.ShapeDtypeStruct
    vm = pl.BlockSpec(memory_space=VM)
    return pl.pallas_call(
        input_kernel, out_shape=(S((rows, d), BF), S((8, d), F32)),
        in_specs=[vm] * 9, out_specs=(vm,) * 2,
        compiler_params=pltpu.CompilerParams(vmem_limit_bytes=32 * 2**20),
        cost_estimate=pl.CostEstimate(flops=2 * d**3 * 3, bytes_accessed=12 * 2**20, transcendentals=10**4),
        name="input_back",
    )(gq, gk, gv, wq, wk, wv, x, gm, gain)

def layer_kernel(k, *refs):
    acts, rws = refs[:k], refs[k:2 * k]
    middle, bias, out_o = refs[2 * k:]
    rows = middle.shape[0]
    for r in range(0, rows, 256):
        rs = slice(r, r + 256)
        total = sum(dot(a[rs, :], w[...]) for a, w in zip(acts, rws))
        out_o[rs, :] = (middle[rs, :] + total + row(bias)).astype(BF)

def layer_end(acts, rws, middle, bias):
    rows, d = middle.shape
    k = len(acts)
    vm = pl.BlockSpec(memory_space=VM)
    return pl.pallas_call(
        functools.partial(layer_kernel, k), out_shape=jax.ShapeDtypeStruct((rows, d), BF),
        in_specs=[vm] * (2 * k + 2), out_specs=vm,
        compiler_params=pltpu.CompilerParams(vmem_limit_bytes=32 * 2**20),
        cost_estimate=pl.CostEstimate(flops=2 * rows * d * sum(w.shape[0] for w in rws), bytes_accessed=12 * 2**20, transcendentals=0),
        name="layer_end",
    )(*acts, *rws, middle, bias)


def flip(value, axis, bit, size):
    return lax.ppermute(value, axis, [(i, i ^ bit) for i in range(size)])

def bits_below(size):
    return [1 << i for i in range(size.bit_length() - 1)]

class Layout:
    def __init__(self, mesh):
        self.nb, self.nt = mesh.shape["batch"], mesh.shape["tp"]
        self.tp = [("tp", b) for b in bits_below(self.nt)]
        self.batch = [("batch", b) for b in bits_below(self.nb)[1:]]
        self.lane_bits = (self.tp + self.batch, self.batch[:1] + self.tp + self.batch[1:])

    def swap(self, value, level):
        axis, bit = level
        return flip(value, axis, bit, self.nb if axis == "batch" else self.nt)

    def core(self, value):
        return flip(value, "batch", 1, self.nb)

def code_of(levels, place):
    out = jnp.int32(0)
    for axis, bit in levels:
        out = out * 2 + (place[axis] // bit) % 2
    return out

def add(a, b):
    return (a.astype(F32) + b.astype(F32)).astype(BF)

def halve(lay, value, level):
    n = value.shape[0] // 2
    return add(value[:n], lay.swap(value[n:], level))

def scatter_width(levels, rows, least=48):
    n = 0
    while n < len(levels) and rows % 2 == 0 and rows // 2 >= least and (rows // 2) % 16 == 0:
        rows //= 2
        n += 1
    return n

def finish_ffn_kernel(pieces, meta, m0, m1, t0, t1, *rest):
    ghw_o, grw_o, mine, theirs = rest[-4:]
    code, core = meta[1], meta[0]
    half = pieces // 2
    step = m0.shape[0] // half
    for p in range(pieces):
        off = pl.multiple_of(jnp.bitwise_xor(p, code) * step, 16)
        src = slice((p % half) * step, (p % half + 1) * step)
        mine[pl.ds(off, step), :] = (m0 if p < half else m1)[src, :]
        theirs[pl.ds(off, step), :] = (t0 if p < half else t1)[src, :]
    first = (core == 0).astype(F32)
    a, b = mine[...].astype(F32), theirs[...].astype(F32)
    ghw_o[...] = jnp.where(core == 0, a, b)
    grw_o[...] = jnp.where(core == 0, b, a).T

def finish_ffn(meta, pieces, parts, k, shard, before):
    d, width = 2 * parts[0].shape[0], parts[0].shape[1]
    S = jax.ShapeDtypeStruct
    vm = pl.BlockSpec(memory_space=VM)
    sm = pl.BlockSpec(memory_space=pltpu.SMEM)
    extra = [] if before is None else list(before)
    return pl.pallas_call(
        functools.partial(finish_ffn_kernel, pieces), grid=(1,),
        out_shape=(S((d, shard), F32), S((shard, d), F32)),
        in_specs=[sm] + [vm] * 4 + [pl.BlockSpec(memory_space=pl.ANY)] * len(extra),
        out_specs=(pl.BlockSpec((d, width), lambda i: (0, k)), pl.BlockSpec((width, d), lambda i: (k, 0))),
        scratch_shapes=[VM((d, width), BF)] * 2,
        input_output_aliases={5: 0, 6: 1} if extra else {},
        compiler_params=pltpu.CompilerParams(vmem_limit_bytes=32 * 2**20),
        cost_estimate=pl.CostEstimate(flops=0, bytes_accessed=12 * d * width, transcendentals=0),
        name="finish_ffn",
    )(meta, *parts, *extra)

def finish_pair_kernel(pieces, cut, meta, *refs):
    parts, (first_o, second_o, mine, theirs) = refs[:-4], refs[-4:]
    half = pieces // 2
    for lane, cs in enumerate((slice(0, cut), slice(cut, None))):
        code = meta[2 + lane]
        m0, m1, t0, t1 = parts[4 * lane:4 * lane + 4]
        step = m0.shape[0] // half
        for p in range(pieces):
            off = pl.multiple_of(jnp.bitwise_xor(p, code) * step, 16)
            src = slice((p % half) * step, (p % half + 1) * step)
            mine[pl.ds(off, step), cs] = (m0 if p < half else m1)[src, :]
            theirs[pl.ds(off, step), cs] = (t0 if p < half else t1)[src, :]
    a, b = mine[...].astype(F32), theirs[...].astype(F32)
    first_o[...] = jnp.where(meta[0] == 0, a, b)
    second_o[...] = jnp.where(meta[0] == 0, b, a)

def finish_pair(meta, pieces, cut, parts, d):
    S = jax.ShapeDtypeStruct
    vm = pl.BlockSpec(memory_space=VM)
    sm = pl.BlockSpec(memory_space=pltpu.SMEM)
    whole = pl.BlockSpec((d, d), lambda i: (0, 0))
    return pl.pallas_call(
        functools.partial(finish_pair_kernel, pieces, cut), grid=(1,),
        out_shape=(S((d, d), F32),) * 2,
        in_specs=[sm] + [vm] * 8, out_specs=(whole, whole),
        scratch_shapes=[VM((d, d), BF)] * 2,
        compiler_params=pltpu.CompilerParams(vmem_limit_bytes=32 * 2**20),
        cost_estimate=pl.CostEstimate(flops=0, bytes_accessed=12 * d * d, transcendentals=0),
        name="finish_pair",
    )(meta, *parts)

def reduce_ffn(lay, keeps, recvs, cut):
    x = lay.batch[0]
    nt = len(keeps)
    d = keeps[0].shape[0]
    low, high = slice(0, d // 2), slice(d // 2, d)
    left = [add(a[:, :cut], b[:, :cut]) for a, b in zip(keeps, recvs)]
    right_send = jnp.concatenate([add(a[high, cut:], b[high, cut:]) for a, b in zip(keeps, recvs)], axis=0)
    right = jnp.concatenate([add(a[low, cut:], b[low, cut:]) for a, b in zip(keeps, recvs)], axis=0)
    right = add(right, lay.swap(right_send, x))
    right = [right[j * (d // 2):(j + 1) * (d // 2)] for j in range(nt)]
    for level in reversed(lay.tp):
        bit = level[1]
        left = [add(left[j], lay.swap(left[j | bit], level)) for j in range(bit)]
        right = [add(right[j], lay.swap(right[j | bit], level)) for j in range(bit)]
    left = halve(lay, left[0], x)
    held = jnp.concatenate([left, right[0]], axis=1)
    for level in lay.batch[1:]:
        held = halve(lay, held, level)
    for level in reversed(lay.batch[1:]):
        held = jnp.concatenate([held, lay.swap(held, level)], axis=0)
    other = lay.swap(held, x)
    return held, other, lay.core(held), lay.core(other)

def reduce_pair(lay, keep, recv, cut):
    d = keep.shape[0]
    lanes = []
    n = scatter_width(lay.lane_bits[0], d)
    join = 1 + len(lay.tp)
    for bits, cs in zip(lay.lane_bits, (slice(0, cut), slice(cut, None))):
        half = d // 2
        held = add(add(keep[:half, cs], recv[:half, cs]), lay.swap(add(keep[half:, cs], recv[half:, cs]), bits[0]))
        for level in bits[1:min(n, join)]:
            held = halve(lay, held, level)
        lanes.append(held)
    held = jnp.concatenate(lanes, axis=1)
    rest = lay.lane_bits[0][join:]
    back = min(n, join)
    for i, level in enumerate(rest):
        held = halve(lay, held, level) if join + i < n else add(held, lay.swap(held, level))
    assert n >= join or True
    for i, level in reversed(list(enumerate(rest))):
        if join + i < n:
            held = jnp.concatenate([held, lay.swap(held, level)], axis=0)
    out = []
    for bits, cs in zip(lay.lane_bits, (slice(0, cut), slice(cut, None))):
        part = held[:, cs]
        for level in reversed(bits[1:back]):
            part = jnp.concatenate([part, lay.swap(part, level)], axis=0)
        other = lay.swap(part, bits[0])
        out += [part, other, lay.core(part), lay.core(other)]
    return out

def on_device(
    lay,
    inputs,
    cotangent,
    zinc_lengths,
    pubchem_lengths,
    feature_stack,
    train_step,
    redraw_interval,
    attn_gain,
    attn_shift,
    query_weight,
    query_bias,
    key_weight,
    key_bias,
    value_weight,
    value_bias,
    output_weight,
    output_bias,
    ffn_gain,
    ffn_shift,
    hidden_weight,
    hidden_bias,
    return_weight,
    return_bias,
):
    nt = lay.nt
    d, shard = hidden_weight.shape
    width = min(768, shard)
    chunks = shard // width
    place = {"batch": lax.axis_index("batch"), "tp": lax.axis_index("tp")}
    core = place["batch"] % 2
    n_pair = scatter_width(lay.lane_bits[0], d)
    quarter = place["batch"] % 4
    meta = jnp.stack([
        core, code_of(lay.batch, place), code_of(lay.lane_bits[0][:n_pair], place),
        code_of(lay.lane_bits[1][:n_pair], place), quarter,
    ]).astype(jnp.int32)
    pick = train_step[0] // redraw_interval[0] % feature_stack.shape[0]
    fp = lax.dynamic_index_in_dim(feature_stack, pick, 0, keepdims=False)
    proj_hi, proj_lo = projection_blocks(fp)
    cos, sin = rotary_const()

    gathered = {}
    for k in range(chunks):
        hw = lax.dynamic_slice(hidden_weight, (quarter * (d // 4), k * width), (d // 4, width))
        rw = lax.dynamic_slice(return_weight, (k * width + quarter * (width // 4), 0), (width // 4, d))
        hb = hidden_bias[k * width:(k + 1) * width]
        pool = {0: (hw, rw, hb)}
        for level in lay.tp:
            for j in list(pool):
                pool[j | level[1]] = tuple(lay.swap(v, level) for v in pool[j])
        for j in range(1, nt):
            hw, rw, hb = pool[j]
            x = lay.batch[0]
            hw2, rw2 = lay.swap(hw, x), lay.swap(rw, x)
            gathered[j, k] = ([hw, lay.core(hw), hw2, lay.core(hw2)], [rw, lay.core(rw), rw2, lay.core(rw2)], hb)

    (n1, n1t, xq, xk, v, fq, fk, state, att, attt, middle, n2, n2t) = attend_fwd(
        inputs, zinc_lengths, pubchem_lengths, attn_gain, attn_shift, query_weight, query_bias, key_weight, key_bias,
        value_weight, value_bias, output_weight, output_bias, ffn_gain, ffn_shift, proj_hi, proj_lo, cos, sin)
    cott = cotangent.T
    acts, slopes, hws, rws, biases, ffn_parts = [], [], [], [], {}, []
    cut = (width // 256) * 128
    for k in range(chunks):
        keeps, recvs = {}, {}
        for j in list(range(1, nt)) + [0]:
            if j:
                hw4, rw4, hb = gathered[j, k]
                send, keep, act, gh, gb, hw, rw = ffn_chunk(meta, 2 ** len(lay.batch), n2, n2t, cotangent, cott, hw4, rw4, hb, 0)
            else:
                send, keep, act, gh, gb = ffn_chunk(meta, 2 ** len(lay.batch), n2, n2t, cotangent, cott, [hidden_weight], [return_weight],
                                                    hidden_bias[k * width:(k + 1) * width], k)
                hw, rw = hidden_weight[:, k * width:(k + 1) * width], return_weight[k * width:(k + 1) * width]
            acts.append(act)
            slopes.append(gh)
            hws.append(hw)
            rws.append(rw)
            biases[j, k] = gb[0]
            keeps[j], recvs[j] = keep, lay.core(send)
        ffn_parts.append(reduce_ffn(lay, [keeps[j] for j in range(nt)], [recvs[j] for j in range(nt)], cut))
    gm, gb, gatt, vec1 = mid(slopes, hws, middle, cotangent, output_weight, ffn_gain)
    gq, gk, gv, send_a, keep_a, send_b, keep_b, vec2 = attend_bwd(
        meta, n_pair, zinc_lengths, pubchem_lengths, gatt, gb, xq, xk, v, fq, fk, state, n1t, attt, proj_hi, cos, sin)
    pair_a = reduce_pair(lay, keep_a, lay.core(send_a), d // 2)
    pair_b = reduce_pair(lay, keep_b, lay.core(send_b), d // 2)
    input_grad, vec3 = input_back(gq, gk, gv, query_weight, key_weight, value_weight, inputs, gm, attn_gain)
    layer_out = layer_end(acts, rws, middle, return_bias)

    vectors = jnp.concatenate([vec1[:4], vec2[:3], vec3[:2]], axis=0).reshape(-1)
    hidden = {j: jnp.concatenate([biases[j, k] for k in range(chunks)]) for j in range(nt)}
    for level in reversed(lay.tp):
        bit = level[1]
        got = lay.swap(jnp.concatenate([vectors] + [hidden[j | bit] for j in range(bit)]), level)
        vectors = vectors + got[:vectors.shape[0]]
        hidden = {j: hidden[j] + got[vectors.shape[0] + j * shard:vectors.shape[0] + (j + 1) * shard] for j in range(bit)}
    small = jnp.concatenate([vectors, hidden[0]])
    for level in [("batch", 1)] + lay.batch:
        small = small + lay.swap(small, level)
    vecs = small[:9 * d].reshape(9, d)
    grad_hidden_bias = small[9 * d:]

    ffn_out = None
    for k in range(chunks):
        ffn_out = finish_ffn(meta, 2 ** len(lay.batch), ffn_parts[k], k, shard, ffn_out)
    gwo, gwv = finish_pair(meta, 2 ** n_pair, d // 2, pair_a, d)
    gwq, gwk = finish_pair(meta, 2 ** n_pair, d // 2, pair_b, d)
    return (layer_out, input_grad, vecs[7], vecs[8], gwq, vecs[4], gwk, vecs[5], gwv, vecs[6], gwo, vecs[2],
            vecs[0], vecs[1], ffn_out[0], grad_hidden_bias, ffn_out[1], vecs[3])

def solution(mesh):
    rows, whole, hidden = P(("batch", "tp"), None), P(), P(None, "tp")
    return jax.shard_map(
        functools.partial(on_device, Layout(mesh)),
        mesh=mesh,
        in_specs=(rows, rows, P(("batch", "tp")), P(("batch", "tp"))) + (whole,) * 15 + (hidden, P("tp"), P("tp", None), whole),
        out_specs=(rows, rows) + (whole,) * 12 + (hidden, P("tp"), P("tp", None), whole),
        check_vma=False,
    )
```

time: 652 us -> 405 us (0.62)
  matrix products: 156 us -> 0 us
  Pallas kernels: 0 us -> 105 us
  local copies, waits for them, and re-layouts: 137 us -> 57.3 us
  blocking collectives: 74.6 us -> 0 us
  starting transfers between devices: 0.24 us -> 71.7 us
  waiting for transfers between devices: 197 us -> 146 us
  other arithmetic: 59.2 us -> 16.7 us
  between operations: 17.8 us -> 3.91 us
    dot_general x42 -> x0, matrix products: 156 us -> none  [the longest x6 40.8 us: matmul(): return jnp.dot(left, right, preferred_element_type=jnp.float32)]
    ppermute x0 -> x83, waiting for transfers between devices: none -> 146 us  [flip(): return lax.ppermute(value, axis, [(i, i ^ bit) for i in range(size)])]
    psum x2 -> x0, waiting for transfers between devices: 143 us -> none  [the longest x1 143 us: on_device(): lax.psum((attention_gain_grad_piece, grad_attn_shift_part, grad_query_wei...]
    pallas_call x0 -> x13, Pallas kernels: none -> 105 us  [the longest x4 27.8 us: ffn_chunk(): pl.pallas_call(functools.partial(ffn_kernel, pieces, count, at), out_shap...]
    psum x2 -> x0, blocking collectives: 74.6 us -> none  [the longest x1 40.1 us: on_device(): lax.psum((attention_gain_grad_piece, grad_attn_shift_part, grad_query_wei...]
    ppermute x0 -> x83, starting transfers between devices: none -> 71.7 us  [flip(): return lax.ppermute(value, axis, [(i, i ^ bit) for i in range(size)])]
    all_gather x2 -> x0, waiting for transfers between devices: 48.8 us -> none  [the longest x1 38.1 us: on_device(): gathered = lax.all_gather(normed_two_low, 'tp', axis=0, tiled=True)]
    reshape x13 -> x1, local copies, waits for them, and re-layouts: 45.9 us -> 0.6 us  [on_device(): jnp.concatenate([vec1[:4], vec2[:3], vec3[:2]], axis=0).reshape(-1)]
  transfers between devices with their start and end apart: 6 -> 83, of which waited for: 4 -> 34; matrix products, arithmetic and copies ran while one was open for 29% -> 6% of each run, Pallas kernels for 0% -> 14%
where the time goes in v1:
time: 405 us; the launch traced here: 401 us
  waiting for transfers between devices  146 us (36%)
  Pallas kernels  105 us (26%)
  starting transfers between devices  71.7 us (18%)
  local copies, waits for them, and re-layouts  57.3 us (14%)
  other arithmetic  16.7 us (4%)
    ppermute x83, waiting for transfers between devices, flip(): return lax.ppermute(value, axis, [(i, i ^ bit) for i in range(size)])  146 us
    ppermute x83, starting transfers between devices, flip(): return lax.ppermute(value, axis, [(i, i ^ bit) for i in range(size)])  71.7 us
    unnamed x201, local copies, waits for them, and re-layouts  47.4 us
    pallas_call x4, Pallas kernels, ffn_chunk(): pl.pallas_call(functools.partial(ffn_kernel, pieces, count, at), out_shap...  27.8 us
    pallas_call x1, Pallas kernels, attend_fwd(): pl.pallas_call(functools.partial(attend_fwd_kernel, zm, pm), out_shape=ou...  21.7 us
    pallas_call x1, Pallas kernels, attend_bwd(): pl.pallas_call(functools.partial(attend_bwd_kernel, zm, pm, 2 ** n_pair),...  20.7 us
    pallas_call x1, Pallas kernels, mid(): pl.pallas_call(functools.partial(mid_kernel, k), out_shape=outs, in_specs...  12.1 us
  transfers between devices with their start and end apart: 83, of which 34 were waited for; matrix products, arithmetic and copies ran while one was open for 6% of the time, Pallas kernels for 14%

profile of v1, /device:TPU:0, one launch (start us, length us, event | category | flops | bytes accessed | tf_op | source)
XLA Modules:
  0.0 401.2 jit_solution(15550593733224246718)
XLA Ops:
  2.6 3.0 collective-permute-start.1
  8.1 2.0 collective-permute-start.9
  29.0 21.7 %attend_fwd.1 = (bf16[768,768]{1,0:T(8,128)(2,1)}, bf16[768,768]{1,0:T(8,128)(2,1)S(1)}, bf16[768,768]{1,0:T(8,128)(2,1)S(1)}, bf16[768,768]{1,0:T(8,128)(2,1)S(...) custom-call(s32[4]{0:T(128)S(1)} %copy-done.49, ...), custom_call_target="tpu_custom_call" | custom-call | flops 4529848320 | bytes 12582912 | tf_op jit(solution)/shard_map/attend_fwd/pallas_call | solution.py:144
  50.8 6.5 %ffn_chunk.7 = (bf16[768,768]{1,0:T(8,128)(2,1)S(1)}, bf16[768,768]{1,0:T(8,128)(2,1)S(1)}, bf16[768,768]{1,0:T(8,128)(2,1)S(1)}, bf16[768,768]{1,0:T(8,128)(2,1)S(1)}, f32[1,768]{1,0:T(1,128)S(1)}) custom-call(s32[5]{0:T(128)S(1)} %stack.23.meta, bf16[768,768]{1,0:T(8,128)(2,1)S(1)} %get-tuple-element.75.n2, bf16[768,768]{1,0:T(8,128)(2,1)S(1)} %get-tuple-element.76.n2t, ...), custom_call_target="tpu_custom_call" | custom-call | flops 3623878656 | bytes 6291456 | tf_op jit(solution)/shard_map/ffn_chunk/pallas_call | solution.py:216
  65.1 6.4 %ffn_chunk.5 = (bf16[768,768]{1,0:T(8,128)(2,1)S(1)}, bf16[768,768]{1,0:T(8,128)(2,1)S(1)}, bf16[768,768]{1,0:T(8,128)(2,1)S(1)}, bf16[768,768]{1,0:T(8,128)(2,1)S(1)}, f32[1,768]{1,0:T(1,128)S(1)}) custom-call(s32[5]{0:T(128)S(1)} %stack.23.meta, bf16[768,768]{1,0:T(8,128)(2,1)S(1)} %get-tuple-element.75.n2, bf16[768,768]{1,0:T(8,128)(2,1)S(1)} %get-tuple-element.76.n2t, ...), custom_call_target="tpu_custom_call" | custom-call | flops 3623878656 | bytes 6291456 | tf_op jit(solution)/shard_map/ffn_chunk/pallas_call | solution.py:216
  73.3 4.7 %collective-permute-done.12.refs_2_ = bf16[192,768]{1,0:T(8,128)(2,1)S(1)} collective-permute-done((bf16[192,768]{1,0:T(8,128)(2,1)}, bf16[192,768]{1,0:T(8,128)(2,1)S(1)}, u32[]{:S(2)}, u32[]{:S(2)}) %collective-permute-start.12) | collective-permute-done | bytes 294944 | tf_op jit(solution)/shard_map/ppermute | solution.py:392
  78.0 6.3 %collective-permute-done.16.refs_6_ = bf16[192,768]{1,0:T(8,128)(2,1)S(1)} collective-permute-done((bf16[192,768]{1,0:T(8,128)(2,1)}, bf16[192,768]{1,0:T(8,128)(2,1)S(1)}, u32[]{:S(2)}, u32[]{:S(2)}) %collective-permute-start.16) | collective-permute-done | bytes 294944 | tf_op jit(solution)/shard_map/ppermute | solution.py:392
  86.0 2.2 collective-permute-done.7.refs_6_
  89.6 7.4 %ffn_chunk.6 = (bf16[768,768]{1,0:T(8,128)(2,1)S(1)}, bf16[768,768]{1,0:T(8,128)(2,1)S(1)}, bf16[768,768]{1,0:T(8,128)(2,1)S(1)}, bf16[768,768]{1,0:T(8,128)(2,1...) custom-call(s32[5]{0:T(128)S(1)} %stack.23.meta, ...), custom_call_target="tpu_custom_call" | custom-call | flops 3623878656 | bytes 6291456 | tf_op jit(solution)/shard_map/ffn_chunk/pallas_call | solution.py:216
  110.2 7.5 %ffn_chunk.4 = (bf16[768,768]{1,0:T(8,128)(2,1)S(1)}, bf16[768,768]{1,0:T(8,128)(2,1)S(1)}, bf16[768,768]{1,0:T(8,128)(2,1)S(1)}, bf16[768,768]{1,0:T(8,128)(2,1...) custom-call(s32[5]{0:T(128)S(1)} %stack.23.meta, ...), custom_call_target="tpu_custom_call" | custom-call | flops 3623878656 | bytes 6291456 | tf_op jit(solution)/shard_map/ffn_chunk/pallas_call | solution.py:216
  139.2 12.1 %mid.1 = (f32[768,768]{1,0:T(8,128)}, bf16[768,768]{1,0:T(8,128)(2,1)S(1)}, f32[768,768]{1,0:T(8,128)}, f32[8,768]{1,0:T(8,128)S(1)}) custom-call(bf16[768,768]{1,0:T(8,128)(2,1)S(1)} %copy-done.85, bf16[768,768]{1,0:T(8,128)(2,1)S(1)} %copy-done.79, bf16[768,768]{1,0:T(8,128)(2,1)S(1)} %copy-done.81, bf16[768,768]{1,0:T(8,128)(2,1)S(1)} %copy-done.73, ...), custom_call_target="tpu_custom_call" | custom-call | flops 5435817984 | bytes 20971520 | tf_op jit(solution)/shard_map/mid/pallas_call | solution.py:253
  151.4 20.7 %attend_bwd.1 = (bf16[768,768]{1,0:T(8,128)(2,1)S(1)}, bf16[768,768]{1,0:T(8,128)(2,1)S(1)}, bf16[768,768]{1,0:T(8,128)(2,1)S(1)}, bf16[768,768]{1,0:T(8,128)(2,...) custom-call(s32[5]{0:T(128)S(1)} %stack.23.meta, ...), custom_call_target="tpu_custom_call" | custom-call | flops 5435817984 | bytes 12582912 | tf_op jit(solution)/shard_map/attend_bwd/pallas_call | solution.py:329
  172.2 4.8 %input_back.1 = (bf16[768,768]{1,0:T(8,128)(2,1)}, f32[8,768]{1,0:T(8,128)S(1)}) custom-call(bf16[768,768]{1,0:T(8,128)(2,1)S(1)} %get-tuple-element.100.gq, bf16[768,768]{1,0:T(8,128)(2,1)S(1)} %get-tuple-element.101.gk, bf16[768,768]{1,0:T(8,128)(2,1)S(1)} %get-tuple-element.102.gv, bf16[768,768]{1,0:T(8,128)(2,1)S(1)} %copy-done.4, ...), custom_call_target="tpu_custom_call" | custom-call | flops 2717908992 | bytes 12582912 | tf_op jit(solution)/shard_map/input_back/pallas_call | solution.py:361
  181.4 2.0 collective-permute-done.18
  187.9 2.3 collective-permute-done.20
  192.0 2.2 collective-permute-done.21
  196.2 2.8 collective-permute-start.22
  206.6 3.8 collective-permute-done.24
  212.2 4.6 %collective-permute-done.41 = bf16[384,384]{1,0:T(8,128)(2,1)S(1)} collective-permute-done((bf16[384,384]{1,0:T(8,128)(2,1)S(1)}, bf16[384,384]{1,0:T(8,128)(2,1)S(1)}, u32[]{:S(2)}, u32[]{:S(2)}) %collective-permute-start.41) | collective-permute-done | bytes 294944 | tf_op jit(solution)/shard_map/ppermute | solution.py:392
  218.4 8.4 %collective-permute-done.25 = bf16[192,384]{1,0:T(8,128)(2,1)S(1)} collective-permute-done((bf16[192,384]{1,0:T(8,128)(2,1)S(1)}, bf16[192,384]{1,0:T(8,128)(2,1)S(1)}, u32[]{:S(2)}, u32[]{:S(2)}) %collective-permute-start.25) | collective-permute-done | bytes 147488 | tf_op jit(solution)/shard_map/ppermute | solution.py:392
  228.4 3.9 collective-permute-done.42
  234.5 7.7 %collective-permute-done.43 = bf16[384,384]{1,0:T(8,128)(2,1)S(1)} collective-permute-done((bf16[384,384]{1,0:T(8,128)(2,1)S(1)}, bf16[384,384]{1,0:T(8,128)(2,1)S(1)}, u32[]{:S(2)}, u32[]{:S(2)}) %collective-permute-start.43) | collective-permute-done | bytes 294944 | tf_op jit(solution)/shard_map/ppermute | solution.py:392
  247.6 3.4 collective-permute-done.74
  251.0 2.1 collective-permute-start.62
  253.3 3.6 collective-permute-done.72
  264.5 5.5 %collective-permute-done.28 = bf16[96,768]{1,0:T(8,128)(2,1)S(1)} collective-permute-done((bf16[96,768]{1,0:T(8,128)(2,1)S(1)}, bf16[96,768]{1,0:T(8,128)(2,1)S(1)}, u32[]{:S(2)}, u32[]{:S(2)}) %collective-permute-start.28) | collective-permute-done | bytes 147488 | tf_op jit(solution)/shard_map/ppermute | solution.py:392
  271.2 5.6 %collective-permute-done.45 = bf16[96,768]{1,0:T(8,128)(2,1)S(1)} collective-permute-done((bf16[96,768]{1,0:T(8,128)(2,1)S(1)}, bf16[96,768]{1,0:T(8,128)(2,1)S(1)}, u32[]{:S(2)}, u32[]{:S(2)}) %collective-permute-start.45) | collective-permute-done | bytes 147488 | tf_op jit(solution)/shard_map/ppermute | solution.py:392
  278.5 3.2 collective-permute-start.46
  282.3 2.0 collective-permute-done.73
  287.6 6.1 %collective-permute-done.30 = bf16[48,768]{1,0:T(8,128)(2,1)S(1)} collective-permute-done((bf16[48,768]{1,0:T(8,128)(2,1)S(1)}, bf16[48,768]{1,0:T(8,128)(2,1)S(1)}, u32[]{:S(2)}, u32[]{:S(2)}) %collective-permute-start.30) | collective-permute-done | bytes 73760 | tf_op jit(solution)/shard_map/ppermute | solution.py:392
  293.8 2.1 collective-permute-start.76
  296.0 4.3 %collective-permute-done.31 = bf16[96,768]{1,0:T(8,128)(2,1)S(1)} collective-permute-done((bf16[96,768]{1,0:T(8,128)(2,1)S(1)}, bf16[96,768]{1,0:T(8,128)(2,1)S(1)}, u32[]{:S(2)}, u32[]{:S(2)}) %collective-permute-start.31) | collective-permute-done | bytes 147488 | tf_op jit(solution)/shard_map/ppermute | solution.py:392
  300.8 5.8 %collective-permute-done.48 = bf16[96,768]{1,0:T(8,128)(2,1)S(1)} collective-permute-done((bf16[96,768]{1,0:T(8,128)(2,1)S(1)}, bf16[96,768]{1,0:T(8,128)(2,1)S(1)}, u32[]{:S(2)}, u32[]{:S(2)}) %collective-permute-start.48) | collective-permute-done | bytes 147488 | tf_op jit(solution)/shard_map/ppermute | solution.py:392
  310.2 4.7 %collective-permute-done.64 = bf16[96,768]{1,0:T(8,128)(2,1)S(1)} collective-permute-done((bf16[96,768]{1,0:T(8,128)(2,1)S(1)}, bf16[96,768]{1,0:T(8,128)(2,1)S(1)}, u32[]{:S(2)}, u32[]{:S(2)}) %collective-permute-start.64) | collective-permute-done | bytes 147488 | tf_op jit(solution)/shard_map/ppermute | solution.py:392
  315.7 6.7 %collective-permute-done.77 = bf16[96,768]{1,0:T(8,128)(2,1)S(1)} collective-permute-done((bf16[96,768]{1,0:T(8,128)(2,1)S(1)}, bf16[96,768]{1,0:T(8,128)(2,1)S(1)}, u32[]{:S(2)}, u32[]{:S(2)}) %collective-permute-start.77) | collective-permute-done | bytes 147488 | tf_op jit(solution)/shard_map/ppermute | solution.py:392
  322.5 6.5 %collective-permute-done.65 = bf16[96,768]{1,0:T(8,128)(2,1)S(1)} collective-permute-done((bf16[96,768]{1,0:T(8,128)(2,1)S(1)}, bf16[96,768]{1,0:T(8,128)(2,1)S(1)}, u32[]{:S(2)}, u32[]{:S(2)}) %collective-permute-start.65) | collective-permute-done | bytes 147488 | tf_op jit(solution)/shard_map/ppermute | solution.py:392
  329.0 2.6 collective-permute-start.66
  331.7 4.1 %collective-permute-done.78 = bf16[96,768]{1,0:T(8,128)(2,1)S(1)} collective-permute-done((bf16[96,768]{1,0:T(8,128)(2,1)S(1)}, bf16[96,768]{1,0:T(8,128)(2,1)S(1)}, u32[]{:S(2)}, u32[]{:S(2)}) %collective-permute-start.78) | collective-permute-done | bytes 147488 | tf_op jit(solution)/shard_map/ppermute | solution.py:392
  338.4 5.0 %collective-permute-done.33.refs_1_ = bf16[384,384]{1,0:T(8,128)(2,1)S(1)} collective-permute-done((bf16[384,384]{1,0:T(8,128)(2,1)S(1)}, bf16[384,384]{1,0:T(8,128)(2,1)S(1)}, u32[]{:S(2)}, u32[]{:S(2)}) %collective-permute-start.33) | collective-permute-done | bytes 294944 | tf_op jit(solution)/shard_map/ppermute | solution.py:392
  344.3 2.2 collective-permute-done.79
  350.7 5.8 %collective-permute-done.54.refs_5_ = bf16[384,384]{1,0:T(8,128)(2,1)S(1)} collective-permute-done((bf16[384,384]{1,0:T(8,128)(2,1)S(1)}, bf16[384,384]{1,0:T(8,128)(2,1)S(1)}, u32[]{:S(2)}, u32[]{:S(2)}) %collective-permute-start.54) | collective-permute-done | bytes 294944 | tf_op jit(solution)/shard_map/ppermute | solution.py:392
  358.2 10.9 %collective-permute-done.67.m1 = bf16[384,768]{1,0:T(8,128)(2,1)S(1)} collective-permute-done((bf16[384,768]{1,0:T(8,128)(2,1)S(1)}, bf16[384,768]{1,0:T(8,128)(2,1)S(1)}, u32[]{:S(2)}, u32[]{:S(2)}) %collective-permute-start.67) | collective-permute-done | bytes 589856 | tf_op jit(solution)/shard_map/ppermute | solution.py:392
  369.1 11.3 %collective-permute-done.80.m1 = bf16[384,768]{1,0:T(8,128)(2,1)S(1)} collective-permute-done((bf16[384,768]{1,0:T(8,128)(2,1)S(1)}, bf16[384,768]{1,0:T(8,128)(2,1)S(1)}, u32[]{:S(2)}, u32[]{:S(2)}) %collective-permute-start.80) | collective-permute-done | bytes 589856 | tf_op jit(solution)/shard_map/ppermute | solution.py:392
  381.2 4.8 %layer_end.1 = bf16[768,768]{1,0:T(8,128)(2,1)} custom-call(bf16[768,768]{1,0:T(8,128)(2,1)S(1)} %copy-done.69, bf16[768,768]{1,0:T(8,128)(2,1)S(1)} %copy-done.63, bf16[768,768]{1,0:T(8,128)(2,1)S(1)} %copy-done.65, bf16[768,768]{1,0:T(8,128)(2,1)S(1)} %copy-done.61, bf16[768,768]{1,0:T(8,128)(2,1)S(1)} %copy-done.71, ...), custom_call_target="tpu_custom_call" | custom-call | flops 3623878656 | bytes 12582912 | tf_op jit(solution)/shard_map/layer_end/pallas_call | solution.py:382
  387.3 3.5 finish_pair.2
  390.7 3.5 finish_pair.3
  394.2 3.3 finish_ffn.2
  397.5 3.3 finish_ffn.3
  (434 shorter events, 132.6 us)
Async XLA Ops:
  2.6 59.0 %collective-permute-start.1 = (bf16[192,768]{1,0:T(8,128)(2,1)}, bf16[192,768]{1,0:T(8,128)(2,1)}, u32[]{:S(2)}, u32[]{:S(2)}) collective-permute-start(bf16[192,768]{1,0:T(8,128)(2,1)} %get-tuple-element.151), channel_id=1, source_target_pairs={{0,1},{1,0},{2,3},{3,2},{4,5},{5,4},{6,7},{7,6},{8,9},{9,8},{10,11... | collective-permute-start | bytes 884744 | tf_op jit(solution)/shard_map/ppermute | solution.py:392
  7.5 64.2 %collective-permute-start.5 = (bf16[192,768]{1,0:T(8,128)(2,1)}, bf16[192,768]{1,0:T(8,128)(2,1)}, u32[]{:S(2)}, u32[]{:S(2)}) collective-permute-start(bf16[192,768]{1,0:T(8,128)(2,1)} %get-tuple-element.149), channel_id=1, source_target_pairs={{0,1},{1,0},{2,3},{3,2},{4,5},{5,4},{6,7},{7,6},{8,9},{9,8},{10,11... | collective-permute-start | bytes 884744 | tf_op jit(solution)/shard_map/ppermute | solution.py:392
  8.1 63.5 %collective-permute-start.9 = (bf16[768]{0:T(1024)(128)(2,1)}, bf16[768]{0:T(1024)(128)(2,1)}, u32[]{:S(2)}, u32[]{:S(2)}) collective-permute-start(bf16[768]{0:T(1024)(128)(2,1)} %get-tuple-element.171.hb), channel_id=1, source_target_pairs={{0,1},{1,0},{2,3},{3,2},{4,5},{5,4},{6,7},{7,6},{8,9},{9,8},{10,11... | collective-permute-start | bytes 4616 | tf_op jit(solution)/shard_map/ppermute | solution.py:392
  10.1 53.0 %collective-permute-start.10 = (bf16[192,768]{1,0:T(8,128)(2,1)}, bf16[192,768]{1,0:T(8,128)(2,1)}, u32[]{:S(2)}, u32[]{:S(2)}) collective-permute-start(bf16[192,768]{1,0:T(8,128)(2,1)} %get-tuple-element.150), channel_id=1, source_target_pairs={{0,1},{1,0},{2,3},{3,2},{4,5},{5,4},{6,7},{7,6},{8,9},{9,8},{10,11... | collective-permute-start | bytes 884744 | tf_op jit(solution)/shard_map/ppermute | solution.py:392
  10.1 53.5 %collective-permute-start.14 = (bf16[192,768]{1,0:T(8,128)(2,1)}, bf16[192,768]{1,0:T(8,128)(2,1)}, u32[]{:S(2)}, u32[]{:S(2)}) collective-permute-start(bf16[192,768]{1,0:T(8,128)(2,1)} %get-tuple-element.148), channel_id=1, source_target_pairs={{0,1},{1,0},{2,3},{3,2},{4,5},{5,4},{6,7},{7,6},{8,9},{9,8},{10,11... | collective-permute-start | bytes 884744 | tf_op jit(solution)/shard_map/ppermute | solution.py:392
  61.6 10.6 %collective-permute-start.3 = (bf16[192,768]{1,0:T(8,128)(2,1)}, bf16[192,768]{1,0:T(8,128)(2,1)}, u32[]{:S(2)}, u32[]{:S(2)}) collective-permute-start(bf16[192,768]{1,0:T(8,128)(2,1)} %collective-permute-done.1.refs_0_), channel_id=1, source_target_pairs={{0,4},{2,6},{4,0},{6,2},{8,12},{10,14},{12,8},{14,10},{16,20},{18,... | collective-permute-start | bytes 884744 | tf_op jit(solution)/shard_map/ppermute | solution.py:392
  63.1 15.0 %collective-permute-start.12 = (bf16[192,768]{1,0:T(8,128)(2,1)}, bf16[192,768]{1,0:T(8,128)(2,1)S(1)}, u32[]{:S(2)}, u32[]{:S(2)}) collective-permute-start(bf16[192,768]{1,0:T(8,128)(2,1)} %collective-permute-done.10.refs_0_), channel_id=1, source_target_pairs={{0,4},{2,6},{4,0},{6,2},{8,12},{10,14},{12,8},{14,10},{16,20},{18,... | collective-permute-start | bytes 884744 | tf_op jit(solution)/shard_map/ppermute | solution.py:392
  63.6 20.8 %collective-permute-start.16 = (bf16[192,768]{1,0:T(8,128)(2,1)}, bf16[192,768]{1,0:T(8,128)(2,1)S(1)}, u32[]{:S(2)}, u32[]{:S(2)}) collective-permute-start(bf16[192,768]{1,0:T(8,128)(2,1)} %collective-permute-done.14.refs_4_), channel_id=1, source_target_pairs={{0,4},{2,6},{4,0},{6,2},{8,12},{10,14},{12,8},{14,10},{16,20},{18,... | collective-permute-start | bytes 884744 | tf_op jit(solution)/shard_map/ppermute | solution.py:392
  71.6 16.9 %collective-permute-start.11 = (bf16[192,768]{1,0:T(8,128)(2,1)}, bf16[192,768]{1,0:T(8,128)(2,1)S(1)}, u32[]{:S(2)}, u32[]{:S(2)}) collective-permute-start(bf16[192,768]{1,0:T(8,128)(2,1)} %collective-permute-done.10.refs_0_), channel_id=1, source_target_pairs={{0,2},{2,0},{4,6},{6,4},{8,10},{10,8},{12,14},{14,12},{16,18},{18,... | collective-permute-start | bytes 884744 | tf_op jit(solution)/shard_map/ppermute | solution.py:392
  71.7 16.8 %collective-permute-start.15 = (bf16[192,768]{1,0:T(8,128)(2,1)}, bf16[192,768]{1,0:T(8,128)(2,1)S(1)}, u32[]{:S(2)}, u32[]{:S(2)}) collective-permute-start(bf16[192,768]{1,0:T(8,128)(2,1)} %collective-permute-done.14.refs_4_), channel_id=1, source_target_pairs={{0,2},{2,0},{4,6},{6,4},{8,10},{10,8},{12,14},{14,12},{16,18},{18,... | collective-permute-start | bytes 884744 | tf_op jit(solution)/shard_map/ppermute | solution.py:392
  72.2 16.0 %collective-permute-start.7 = (bf16[192,768]{1,0:T(8,128)(2,1)}, bf16[192,768]{1,0:T(8,128)(2,1)}, u32[]{:S(2)}, u32[]{:S(2)}) collective-permute-start(bf16[192,768]{1,0:T(8,128)(2,1)} %collective-permute-done.5.refs_4_), channel_id=1, source_target_pairs={{0,4},{2,6},{4,0},{6,2},{8,12},{10,14},{12,8},{14,10},{16,20},{18,... | collective-permute-start | bytes 884744 | tf_op jit(solution)/shard_map/ppermute | solution.py:392
  78.0 11.0 %collective-permute-start.13 = (bf16[192,768]{1,0:T(8,128)(2,1)S(1)}, bf16[192,768]{1,0:T(8,128)(2,1)S(1)}, u32[]{:S(2)}, u32[]{:S(2)}) collective-permute-start(bf16[192,768]{1,0:T(8,128)(2,1)S(1)} %collective-permute-done.12.refs_2_), channel_id=1, source_target_pairs={{0,2},{2,0},{4,6},{6,4},{8,10},{10,8},{12,14},{14,12},{16,18},{18,... | collective-permute-start | bytes 884744 | tf_op jit(solution)/shard_map/ppermute | solution.py:392
  88.2 16.9 %collective-permute-start = (bf16[768]{0:T(1024)(128)(2,1)}, bf16[768]{0:T(1024)(128)(2,1)}, u32[]{:S(2)}, u32[]{:S(2)}) collective-permute-start(bf16[768]{0:T(1024)(128)(2,1)} %get-tuple-element.172.hb), channel_id=1, source_target_pairs={{0,1},{1,0},{2,3},{3,2},{4,5},{5,4},{6,7},{7,6},{8,9},{9,8},{10,11... | collective-permute-start | bytes 4616 | tf_op jit(solution)/shard_map/ppermute | solution.py:392
  88.5 16.5 %collective-permute-start.2 = (bf16[192,768]{1,0:T(8,128)(2,1)}, bf16[192,768]{1,0:T(8,128)(2,1)}, u32[]{:S(2)}, u32[]{:S(2)}) collective-permute-start(bf16[192,768]{1,0:T(8,128)(2,1)} %collective-permute-done.1.refs_0_), channel_id=1, source_target_pairs={{0,2},{2,0},{4,6},{6,4},{8,10},{10,8},{12,14},{14,12},{16,18},{18,... | collective-permute-start | bytes 884744 | tf_op jit(solution)/shard_map/ppermute | solution.py:392
  88.5 16.5 %collective-permute-start.6 = (bf16[192,768]{1,0:T(8,128)(2,1)}, bf16[192,768]{1,0:T(8,128)(2,1)}, u32[]{:S(2)}, u32[]{:S(2)}) collective-permute-start(bf16[192,768]{1,0:T(8,128)(2,1)} %collective-permute-done.5.refs_4_), channel_id=1, source_target_pairs={{0,2},{2,0},{4,6},{6,4},{8,10},{10,8},{12,14},{14,12},{16,18},{18,... | collective-permute-start | bytes 884744 | tf_op jit(solution)/shard_map/ppermute | solution.py:392
  89.0 16.0 %collective-permute-start.4 = (bf16[192,768]{1,0:T(8,128)(2,1)}, bf16[192,768]{1,0:T(8,128)(2,1)}, u32[]{:S(2)}, u32[]{:S(2)}) collective-permute-start(bf16[192,768]{1,0:T(8,128)(2,1)} %collective-permute-done.3.refs_2_), channel_id=1, source_target_pairs={{0,2},{2,0},{4,6},{6,4},{8,10},{10,8},{12,14},{14,12},{16,18},{18,... | collective-permute-start | bytes 884744 | tf_op jit(solution)/shard_map/ppermute | solution.py:392
  89.1 16.0 %collective-permute-start.8 = (bf16[192,768]{1,0:T(8,128)(2,1)}, bf16[192,768]{1,0:T(8,128)(2,1)}, u32[]{:S(2)}, u32[]{:S(2)}) collective-permute-start(bf16[192,768]{1,0:T(8,128)(2,1)} %collective-permute-done.7.refs_6_), channel_id=1, source_target_pairs={{0,2},{2,0},{4,6},{6,4},{8,10},{10,8},{12,14},{14,12},{16,18},{18,... | collective-permute-start | bytes 884744 | tf_op jit(solution)/shard_map/ppermute | solution.py:392
  180.8 13.4 %collective-permute-start.57 = (bf16[768,768]{1,0:T(8,128)(2,1)}, bf16[768,768]{1,0:T(8,128)(2,1)}, u32[]{:S(2)}, u32[]{:S(2)}) collective-permute-start(bf16[768,768]{1,0:T(8,128)(2,1)} %copy-done.34), channel_id=1, source_target_pairs={{0,2},{2,0},{4,6},{6,4},{8,10},{10,8},{12,14},{14,12},{16,18},{18,... | collective-permute-start | bytes 3538952 | tf_op jit(solution)/shard_map/ppermute | solution.py:392
  180.8 15.3 %collective-permute-start.70 = (bf16[768,768]{1,0:T(8,128)(2,1)}, bf16[768,768]{1,0:T(8,128)(2,1)}, u32[]{:S(2)}, u32[]{:S(2)}) collective-permute-start(bf16[768,768]{1,0:T(8,128)(2,1)} %copy-done.35), channel_id=1, source_target_pairs={{0,2},{2,0},{4,6},{6,4},{8,10},{10,8},{12,14},{14,12},{16,18},{18,... | collective-permute-start | bytes 3538952 | tf_op jit(solution)/shard_map/ppermute | solution.py:392
  185.0 15.3 %collective-permute-start.23 = (bf16[768,768]{1,0:T(8,128)(2,1)}, bf16[768,768]{1,0:T(8,128)(2,1)S(1)}, u32[]{:S(2)}, u32[]{:S(2)}) collective-permute-start(bf16[768,768]{1,0:T(8,128)(2,1)} %copy-done.39), channel_id=1, source_target_pairs={{0,2},{2,0},{4,6},{6,4},{8,10},{10,8},{12,14},{14,12},{16,18},{18,... | collective-permute-start | bytes 3538952 | tf_op jit(solution)/shard_map/ppermute | solution.py:392
  185.5 16.5 %collective-permute-start.40 = (bf16[768,768]{1,0:T(8,128)(2,1)}, bf16[768,768]{1,0:T(8,128)(2,1)S(1)}, u32[]{:S(2)}, u32[]{:S(2)}) collective-permute-start(bf16[768,768]{1,0:T(8,128)(2,1)} %copy-done.38), channel_id=1, source_target_pairs={{0,2},{2,0},{4,6},{6,4},{8,10},{10,8},{12,14},{14,12},{16,18},{18,... | collective-permute-start | bytes 3538952 | tf_op jit(solution)/shard_map/ppermute | solution.py:392
  194.2 10.4 %collective-permute-start.71 = (bf16[768,768]{1,0:T(8,128)(2,1)}, bf16[768,768]{1,0:T(8,128)(2,1)S(1)}, u32[]{:S(2)}, u32[]{:S(2)}) collective-permute-start(bf16[768,768]{1,0:T(8,128)(2,1)} %copy-done.37), channel_id=1, source_target_pairs={{0,2},{2,0},{4,6},{6,4},{8,10},{10,8},{12,14},{14,12},{16,18},{18,... | collective-permute-start | bytes 3538952 | tf_op jit(solution)/shard_map/ppermute | solution.py:392
  196.2 140.9 %collective-permute-start.22 = (f32[8448]{0:T(1024)S(1)}, f32[8448]{0:T(1024)S(1)}, u32[]{:S(2)}, u32[]{:S(2)}) collective-permute-start(f32[8448]{0:T(1024)S(1)} %add.248), channel_id=1, source_target_pairs={{0,16},{2,18},{4,20},{6,22},{8,24},{10,26},{12,28},{14,30},{16,0},... | collective-permute-start | bytes 101384 | tf_op jit(solution)/shard_map/ppermute | solution.py:392
  202.1 14.6 %collective-permute-start.41 = (bf16[384,384]{1,0:T(8,128)(2,1)S(1)}, bf16[384,384]{1,0:T(8,128)(2,1)S(1)}, u32[]{:S(2)}, u32[]{:S(2)}) collective-permute-start(bf16[384,384]{1,0:T(8,128)(2,1)S(1)} %add_convert_fusion.26), channel_id=1, source_target_pairs={{0,1},{1,0},{2,3},{3,2},{4,5},{5,4},{6,7},{7,6},{8,9},{9,8},{10,11... | collective-permute-start | bytes 884744 | tf_op jit(solution)/shard_map/ppermute | solution.py:392
  202.9 41.0 %collective-permute-start.61 = (bf16[768,384]{1,0:T(8,128)(2,1)S(1)}, bf16[768,384]{1,0:T(8,128)(2,1)S(1)}, u32[]{:S(2)}, u32[]{:S(2)}) collective-permute-start(bf16[768,384]{1,0:T(8,128)(2,1)S(1)} %pad_maximum_fusion.1), channel_id=1, source_target_pairs={{0,4},{2,6},{4,0},{6,2},{8,12},{10,14},{12,8},{14,10},{16,20},{18,... | collective-permute-start | bytes 1769480 | tf_op jit(solution)/shard_map/ppermute | solution.py:392
  204.6 40.1 %collective-permute-start.59 = (bf16[768,384]{1,0:T(8,128)(2,1)S(1)}, bf16[768,384]{1,0:T(8,128)(2,1)S(1)}, u32[]{:S(2)}, u32[]{:S(2)}) collective-permute-start(bf16[768,384]{1,0:T(8,128)(2,1)S(1)} %add_convert_fusion.6), channel_id=1, source_target_pairs={{0,1},{1,0},{2,3},{3,2},{4,5},{5,4},{6,7},{7,6},{8,9},{9,8},{10,11... | collective-permute-start | bytes 1769480 | tf_op jit(solution)/shard_map/ppermute | solution.py:392
  210.6 23.2 %collective-permute-start.26 = (bf16[384,384]{1,0:T(8,128)(2,1)S(1)}, bf16[384,384]{1,0:T(8,128)(2,1)S(1)}, u32[]{:S(2)}, u32[]{:S(2)}) collective-permute-start(bf16[384,384]{1,0:T(8,128)(2,1)S(1)} %get-tuple-element.143), channel_id=1, source_target_pairs={{0,4},{2,6},{4,0},{6,2},{8,12},{10,14},{12,8},{14,10},{16,20},{18,... | collective-permute-start | bytes 884744 | tf_op jit(solution)/shard_map/ppermute | solution.py:392
  233.8 17.2 %collective-permute-start.74 = (bf16[768,384]{1,0:T(8,128)(2,1)S(1)}, bf16[768,384]{1,0:T(8,128)(2,1)S(1)}, u32[]{:S(2)}, u32[]{:S(2)}) collective-permute-start(bf16[768,384]{1,0:T(8,128)(2,1)S(1)} %pad_maximum_fusion.3), channel_id=1, source_target_pairs={{0,4},{2,6},{4,0},{6,2},{8,12},{10,14},{12,8},{14,10},{16,20},{18,... | collective-permute-start | bytes 1769480 | tf_op jit(solution)/shard_map/ppermute | solution.py:392
  242.2 14.7 %collective-permute-start.72 = (bf16[768,384]{1,0:T(8,128)(2,1)S(1)}, bf16[768,384]{1,0:T(8,128)(2,1)S(1)}, u32[]{:S(2)}, u32[]{:S(2)}) collective-permute-start(bf16[768,384]{1,0:T(8,128)(2,1)S(1)} %add_convert_fusion.2), channel_id=1, source_target_pairs={{0,1},{1,0},{2,3},{3,2},{4,5},{5,4},{6,7},{7,6},{8,9},{9,8},{10,11... | collective-permute-start | bytes 1769480 | tf_op jit(solution)/shard_map/ppermute | solution.py:392
  243.9 16.2 %collective-permute-start.27 = (bf16[192,384]{1,0:T(8,128)(2,1)S(1)}, bf16[192,384]{1,0:T(8,128)(2,1)S(1)}, u32[]{:S(2)}, u32[]{:S(2)}) collective-permute-start(bf16[192,384]{1,0:T(8,128)(2,1)S(1)} %slice.430), channel_id=1, source_target_pairs={{0,1},{1,0},{2,3},{3,2},{4,5},{5,4},{6,7},{7,6},{8,9},{9,8},{10,11... | collective-permute-start | bytes 442376 | tf_op jit(solution)/shard_map/ppermute | solution.py:392
  244.7 18.2 %collective-permute-start.44 = (bf16[192,384]{1,0:T(8,128)(2,1)S(1)}, bf16[192,384]{1,0:T(8,128)(2,1)S(1)}, u32[]{:S(2)}, u32[]{:S(2)}) collective-permute-start(bf16[192,384]{1,0:T(8,128)(2,1)S(1)} %slice.446), channel_id=1, source_target_pairs={{0,1},{1,0},{2,3},{3,2},{4,5},{5,4},{6,7},{7,6},{8,9},{9,8},{10,11... | collective-permute-start | bytes 442376 | tf_op jit(solution)/shard_map/ppermute | solution.py:392
  251.0 27.4 %collective-permute-start.62 = (bf16[384,384]{1,0:T(8,128)(2,1)S(1)}, bf16[384,384]{1,0:T(8,128)(2,1)S(1)}, u32[]{:S(2)}, u32[]{:S(2)}) collective-permute-start(bf16[384,384]{1,0:T(8,128)(2,1)S(1)} %slice.466), channel_id=1, source_target_pairs={{0,1},{1,0},{2,3},{3,2},{4,5},{5,4},{6,7},{7,6},{8,9},{9,8},{10,11... | collective-permute-start | bytes 884744 | tf_op jit(solution)/shard_map/ppermute | solution.py:392
  256.9 21.6 %collective-permute-start.60 = (bf16[384,384]{1,0:T(8,128)(2,1)S(1)}, bf16[384,384]{1,0:T(8,128)(2,1)S(1)}, u32[]{:S(2)}, u32[]{:S(2)}) collective-permute-start(bf16[384,384]{1,0:T(8,128)(2,1)S(1)} %slice.460), channel_id=1, source_target_pairs={{0,4},{2,6},{4,0},{6,2},{8,12},{10,14},{12,8},{14,10},{16,20},{18,... | collective-permute-start | bytes 884744 | tf_op jit(solution)/shard_map/ppermute | solution.py:392
  260.1 21.8 %collective-permute-start.75 = (bf16[384,384]{1,0:T(8,128)(2,1)S(1)}, bf16[384,384]{1,0:T(8,128)(2,1)S(1)}, u32[]{:S(2)}, u32[]{:S(2)}) collective-permute-start(bf16[384,384]{1,0:T(8,128)(2,1)S(1)} %slice.480), channel_id=1, source_target_pairs={{0,1},{1,0},{2,3},{3,2},{4,5},{5,4},{6,7},{7,6},{8,9},{9,8},{10,11... | collective-permute-start | bytes 884744 | tf_op jit(solution)/shard_map/ppermute | solution.py:392
  281.9 24.8 %collective-permute-start.63 = (bf16[192,768]{1,0:T(8,128)(2,1)S(1)}, bf16[192,768]{1,0:T(8,128)(2,1)S(1)}, u32[]{:S(2)}, u32[]{:S(2)}) collective-permute-start(bf16[192,768]{1,0:T(8,128)(2,1)S(1)} %pad_maximum_fusion.6), channel_id=1, source_target_pairs={{0,8},{2,10},{4,12},{6,14},{8,0},{10,2},{12,4},{14,6},{16,24},{18,... | collective-permute-start | bytes 884744 | tf_op jit(solution)/shard_map/ppermute | solution.py:392
  293.8 13.3 %collective-permute-start.76 = (bf16[192,768]{1,0:T(8,128)(2,1)S(1)}, bf16[192,768]{1,0:T(8,128)(2,1)S(1)}, u32[]{:S(2)}, u32[]{:S(2)}) collective-permute-start(bf16[192,768]{1,0:T(8,128)(2,1)S(1)} %pad_maximum_fusion.5), channel_id=1, source_target_pairs={{0,8},{2,10},{4,12},{6,14},{8,0},{10,2},{12,4},{14,6},{16,24},{18,... | collective-permute-start | bytes 884744 | tf_op jit(solution)/shard_map/ppermute | solution.py:392
  295.9 10.7 %collective-permute-start.48 = (bf16[96,768]{1,0:T(8,128)(2,1)S(1)}, bf16[96,768]{1,0:T(8,128)(2,1)S(1)}, u32[]{:S(2)}, u32[]{:S(2)}) collective-permute-start(bf16[96,768]{1,0:T(8,128)(2,1)S(1)} %pad_maximum_fusion.18), channel_id=1, source_target_pairs={{0,8},{2,10},{4,12},{6,14},{8,0},{10,2},{12,4},{14,6},{16,24},{18,... | collective-permute-start | bytes 442376 | tf_op jit(solution)/shard_map/ppermute | solution.py:392
  306.6 22.4 %collective-permute-start.36 = (bf16[192,384]{1,0:T(8,128)(2,1)S(1)}, bf16[192,384]{1,0:T(8,128)(2,1)S(1)}, u32[]{:S(2)}, u32[]{:S(2)}) collective-permute-start(bf16[192,384]{1,0:T(8,128)(2,1)S(1)} %get-tuple-element.156), channel_id=1, source_target_pairs={{0,1},{1,0},{2,3},{3,2},{4,5},{5,4},{6,7},{7,6},{8,9},{9,8},{10,11... | collective-permute-start | bytes 442376 | tf_op jit(solution)/shard_map/ppermute | solution.py:392
  306.7 30.5 %collective-permute-start.49 = (bf16[192,384]{1,0:T(8,128)(2,1)S(1)}, bf16[192,384]{1,0:T(8,128)(2,1)S(1)}, u32[]{:S(2)}, u32[]{:S(2)}) collective-permute-start(bf16[192,384]{1,0:T(8,128)(2,1)S(1)} %get-tuple-element.155), channel_id=1, source_target_pairs={{0,4},{2,6},{4,0},{6,2},{8,12},{10,14},{12,8},{14,10},{16,20},{18,... | collective-permute-start | bytes 442376 | tf_op jit(solution)/shard_map/ppermute | solution.py:392
  308.2 29.0 %collective-permute-start.53 = (bf16[192,384]{1,0:T(8,128)(2,1)S(1)}, bf16[192,384]{1,0:T(8,128)(2,1)S(1)}, u32[]{:S(2)}, u32[]{:S(2)}) collective-permute-start(bf16[192,384]{1,0:T(8,128)(2,1)S(1)} %get-tuple-element.154), channel_id=1, source_target_pairs={{0,1},{1,0},{2,3},{3,2},{4,5},{5,4},{6,7},{7,6},{8,9},{9,8},{10,11... | collective-permute-start | bytes 442376 | tf_op jit(solution)/shard_map/ppermute | solution.py:392
  338.2 10.5 %collective-permute-start.38 = (bf16[384,384]{1,0:T(8,128)(2,1)S(1)}, bf16[384,384]{1,0:T(8,128)(2,1)S(1)}, u32[]{:S(2)}, u32[]{:S(2)}) collective-permute-start(bf16[384,384]{1,0:T(8,128)(2,1)S(1)} %pad_maximum_fusion.9.refs_4_), channel_id=1, source_target_pairs={{0,2},{2,0},{4,6},{6,4},{8,10},{10,8},{12,14},{14,12},{16,18},{18,... | collective-permute-start | bytes 884744 | tf_op jit(solution)/shard_map/ppermute | solution.py:392
  347.5 21.6 %collective-permute-start.67 = (bf16[384,768]{1,0:T(8,128)(2,1)S(1)}, bf16[384,768]{1,0:T(8,128)(2,1)S(1)}, u32[]{:S(2)}, u32[]{:S(2)}) collective-permute-start(bf16[384,768]{1,0:T(8,128)(2,1)S(1)} %pad_maximum_fusion.2.m0), channel_id=1, source_target_pairs={{0,4},{2,6},{4,0},{6,2},{8,12},{10,14},{12,8},{14,10},{16,20},{18,... | collective-permute-start | bytes 1769480 | tf_op jit(solution)/shard_map/ppermute | solution.py:392
  348.7 31.6 %collective-permute-start.80 = (bf16[384,768]{1,0:T(8,128)(2,1)S(1)}, bf16[384,768]{1,0:T(8,128)(2,1)S(1)}, u32[]{:S(2)}, u32[]{:S(2)}) collective-permute-start(bf16[384,768]{1,0:T(8,128)(2,1)S(1)} %pad_maximum_fusion.4.m0), channel_id=1, source_target_pairs={{0,4},{2,6},{4,0},{6,2},{8,12},{10,14},{12,8},{14,10},{16,20},{18,... | collective-permute-start | bytes 1769480 | tf_op jit(solution)/shard_map/ppermute | solution.py:392
  356.5 24.1 %collective-permute-start.52 = (bf16[384,384]{1,0:T(8,128)(2,1)S(1)}, bf16[384,384]{1,0:T(8,128)(2,1)S(1)}, u32[]{:S(2)}, u32[]{:S(2)}) collective-permute-start(bf16[384,384]{1,0:T(8,128)(2,1)S(1)} %collective-permute-done.50.refs_1_), channel_id=1, source_target_pairs={{0,2},{2,0},{4,6},{6,4},{8,10},{10,8},{12,14},{14,12},{16,18},{18,... | collective-permute-start | bytes 884744 | tf_op jit(solution)/shard_map/ppermute | solution.py:392
  357.0 40.5 %collective-permute-start.68 = (bf16[384,768]{1,0:T(8,128)(2,1)S(1)}, bf16[384,768]{1,0:T(8,128)(2,1)S(1)}, u32[]{:S(2)}, u32[]{:S(2)}) collective-permute-start(bf16[384,768]{1,0:T(8,128)(2,1)S(1)} %pad_maximum_fusion.2.m0), channel_id=1, source_target_pairs={{0,2},{2,0},{4,6},{6,4},{8,10},{10,8},{12,14},{14,12},{16,18},{18,... | collective-permute-start | bytes 1769480 | tf_op jit(solution)/shard_map/ppermute | solution.py:392
  358.1 36.1 %collective-permute-start.81 = (bf16[384,768]{1,0:T(8,128)(2,1)S(1)}, bf16[384,768]{1,0:T(8,128)(2,1)S(1)}, u32[]{:S(2)}, u32[]{:S(2)}) collective-permute-start(bf16[384,768]{1,0:T(8,128)(2,1)S(1)} %pad_maximum_fusion.4.m0), channel_id=1, source_target_pairs={{0,2},{2,0},{4,6},{6,4},{8,10},{10,8},{12,14},{14,12},{16,18},{18,... | collective-permute-start | bytes 1769480 | tf_op jit(solution)/shard_map/ppermute | solution.py:392
  369.1 28.4 %collective-permute-start.69 = (bf16[384,768]{1,0:T(8,128)(2,1)S(1)}, bf16[384,768]{1,0:T(8,128)(2,1)S(1)}, u32[]{:S(2)}, u32[]{:S(2)}) collective-permute-start(bf16[384,768]{1,0:T(8,128)(2,1)S(1)} %collective-permute-done.67.m1), channel_id=1, source_target_pairs={{0,2},{2,0},{4,6},{6,4},{8,10},{10,8},{12,14},{14,12},{16,18},{18,... | collective-permute-start | bytes 1769480 | tf_op jit(solution)/shard_map/ppermute | solution.py:392
  380.4 13.8 %collective-permute-start.82 = (bf16[384,768]{1,0:T(8,128)(2,1)S(1)}, bf16[384,768]{1,0:T(8,128)(2,1)S(1)}, u32[]{:S(2)}, u32[]{:S(2)}) collective-permute-start(bf16[384,768]{1,0:T(8,128)(2,1)S(1)} %collective-permute-done.80.m1), channel_id=1, source_target_pairs={{0,2},{2,0},{4,6},{6,4},{8,10},{10,8},{12,14},{14,12},{16,18},{18,... | collective-permute-start | bytes 1769480 | tf_op jit(solution)/shard_map/ppermute | solution.py:392
  (135 other events, 1148.2 us)
